TPU v7x, 32 devices: a whole 2x2x4 slice. The times are simulated.
32 devices in a mesh: parts: 2 (over y), wide: 4 (over z), narrow: 4 (over x, core).
Axes of the slice: x: 2, y: 2, z: 4, core: 2. Of those that a mesh axis runs over, the one named last changes fastest.
Arguments:
- recording: bfloat16 [64, 512, 2048], P(('parts', 'wide'), None, 'narrow'), parts along dimension 0, may hold values from -6 to 6
- offsets: int32 [2, 64], P(None, 'parts'), parts along dimension 1, may hold values from -4 to 4
- center_rows: int32 [8, 4, 32], P(('parts', 'wide'), 'narrow'), parts along dimension 0, may hold values from 0 to 127
- center_cols: int32 [8, 4, 32], P(('parts', 'wide'), 'narrow'), parts along dimension 0, may hold values from 0 to 511
- decays: float32 [8, 4, 32], P(('parts', 'wide'), 'narrow'), parts along dimension 0, may hold values from 0.3 to 0.95
Outputs:
- footprints: bfloat16 [8, 4, 32, 135168], P(('parts', 'wide'), 'narrow'), parts along dimension 0
- traces: float32 [8, 4, 32, 16], P(('parts', 'wide'), 'narrow'), parts along dimension 0
- spikes: float32 [8, 4, 32, 16], P(('parts', 'wide'), 'narrow'), parts along dimension 0
There are 2 independent parts, one for each index of `parts`. A program takes and returns all parts, laid end to end along the dimension named above; each array names one. Nothing has to cross between parts.
All inputs are finite; a program needn't handle non-finite values.
Results may differ from a plain program's by a relative error of at most 0.013.
The roundings to bfloat16 on the way count: a program that leaves them out, or rounds other values in their place, can miss the bound.
Values may be sent and summed in bfloat16 or wider, within the bound.
A program may use at most 128 MiB of HBM per device.

v0:
```python
import jax
import jax.numpy as jnp
from jax import lax
from jax.sharding import PartitionSpec as P

PLANES = 2
VOLUMES = 16
MARGIN = 8
SHIFT_MAX = 4
RADIUS = 12
ITERS = 3


RIDGE = 1.0


def extended(cells, sides, width, closed):
    for axis, dim in sides:
        count = lax.axis_size(axis)
        ends = count if closed else count - 1
        head = lax.slice_in_dim(cells, 0, width, axis=dim)
        tail = lax.slice_in_dim(cells, cells.shape[dim] - width, cells.shape[dim], axis=dim)
        cells = jnp.concatenate(
            [
                lax.ppermute(tail, axis, [(i, (i + 1) % count) for i in range(ends)]),
                cells,
                lax.ppermute(head, axis, [((i + 1) % count, i) for i in range(ends)]),
            ],
            axis=dim,
        )
    return cells


def shifted_frames(with_edges, row_shift, col_shift, rows_out, cols_out):

    def place(single, row_move, col_move):
        return lax.dynamic_slice(
            single, (SHIFT_MAX - row_move, SHIFT_MAX - col_move), (rows_out, cols_out)
        )

    return jax.vmap(place)(with_edges, row_shift, col_shift)


def shards(recording, offsets, center_rows, center_cols, decays):
    frames_dev, height, cols_patch = recording.shape
    wide_count = lax.axis_size("wide")
    rows_patch = height // wide_count
    ext_width = cols_patch + 2 * MARGIN
    first_frame = lax.axis_index("wide") * frames_dev
    own_rows = lax.dynamic_slice_in_dim(offsets[0], first_frame, frames_dev, 0)
    own_cols = lax.dynamic_slice_in_dim(offsets[1], first_frame, frames_dev, 0)
    with_edges = extended(recording, (("narrow", 2),), SHIFT_MAX, True)
    with_edges = jnp.concatenate(
        [with_edges[:, height - SHIFT_MAX :], with_edges, with_edges[:, :SHIFT_MAX]], axis=1
    )
    registered = shifted_frames(with_edges, own_rows, own_cols, height, cols_patch)
    plane_of = (first_frame + jnp.arange(frames_dev, dtype=jnp.int32)) // VOLUMES
    onehot = (jnp.arange(PLANES, dtype=jnp.int32)[:, None] == plane_of[None, :]).astype(
        jnp.bfloat16
    )
    partial_value = jnp.dot(
        onehot, registered.reshape(frames_dev, -1), preferred_element_type=jnp.float32
    )
    partial_value = partial_value.reshape(PLANES, height, cols_patch)
    summed = lax.psum(partial_value, "wide")
    summed = lax.dynamic_slice_in_dim(summed, lax.axis_index("wide") * rows_patch, rows_patch, 1)
    template = summed / VOLUMES
    grouped = lax.all_to_all(registered, "wide", split_axis=1, concat_axis=0, tiled=True)
    observed_low = (
        (
            grouped.reshape(PLANES, VOLUMES, rows_patch, cols_patch).astype(jnp.float32)
            - template[:, None]
        )
        .transpose(1, 0, 2, 3)
        .astype(jnp.bfloat16)
    )
    column_index = lax.axis_index("narrow")
    width_total = cols_patch * lax.axis_size("narrow")
    row_pos = jnp.arange(rows_patch, dtype=jnp.int32).astype(jnp.float32)
    col_pos = jnp.arange(ext_width, dtype=jnp.int32) - MARGIN
    global_col = column_index * cols_patch + col_pos
    inside = ((global_col >= 0) & (global_col < width_total)).astype(jnp.float32)
    rows_center = center_rows[0, 0].astype(jnp.float32)
    cols_center = center_cols[0, 0].astype(jnp.float32)
    row_bump = jnp.maximum(0.0, 1.0 - jnp.abs(row_pos[None, :] - rows_center[:, None]) / RADIUS)
    col_bump = (
        jnp.maximum(
            0.0, 1.0 - jnp.abs(col_pos.astype(jnp.float32)[None, :] - cols_center[:, None]) / RADIUS
        )
        * inside[None, :]
    )
    planar = row_bump[:, :, None] * col_bump[:, None, :]
    comps = planar.shape[0]
    footprints = jnp.broadcast_to(planar[:, None], (comps, PLANES, rows_patch, ext_width)).reshape(
        comps, -1
    )
    support = jnp.broadcast_to(inside, (PLANES, rows_patch, ext_width)).reshape(-1)
    traces = jnp.zeros((comps, VOLUMES), jnp.float32)
    contract = (((0,), (0,)), ((), ()))
    no_pad = ((0, 0), (0, 0), (0, 0))

    def factor_residual(footprints, traces, sides):
        strip_left, strip_right = sides
        own_low = traces.astype(jnp.bfloat16)
        trace_sides = extended(own_low, (("narrow", 1),), VOLUMES, False)
        trace_left = trace_sides[:, :VOLUMES]
        trace_right = trace_sides[:, 2 * VOLUMES :]
        model_ext = lax.dot_general(
            own_low, footprints.astype(jnp.bfloat16), contract, preferred_element_type=jnp.float32
        )
        model_ext = model_ext.reshape(VOLUMES, PLANES, rows_patch, ext_width)
        part_left = lax.dot_general(
            trace_left, strip_left.reshape(comps, -1), contract, preferred_element_type=jnp.float32
        )
        part_left = part_left.reshape(VOLUMES, PLANES, rows_patch, 2 * MARGIN)
        part_right = lax.dot_general(
            trace_right,
            strip_right.reshape(comps, -1),
            contract,
            preferred_element_type=jnp.float32,
        )
        part_right = part_right.reshape(VOLUMES, PLANES, rows_patch, 2 * MARGIN)
        model_ext = model_ext + jnp.pad(part_left, no_pad + ((0, cols_patch),))
        model_ext = model_ext + jnp.pad(part_right, no_pad + ((cols_patch, 0),))
        residual = (observed_ext - model_ext).astype(jnp.bfloat16)
        return residual.reshape(VOLUMES, -1)

    observed_ext = extended(observed_low, (("narrow", 3),), MARGIN, False).astype(jnp.float32)
    for sweep in range(ITERS):
        sides = None
        shaped = footprints.astype(jnp.bfloat16).reshape(comps, PLANES, rows_patch, ext_width)
        bordered = extended(shaped, (("narrow", 3),), 2 * MARGIN, False)
        sides = (bordered[..., : 2 * MARGIN], bordered[..., ext_width + 2 * MARGIN :])
        residual = factor_residual(footprints, traces, sides)
        project = lax.dot_general(
            footprints.astype(jnp.bfloat16),
            residual,
            (((1,), (1,)), ((), ())),
            preferred_element_type=jnp.float32,
        )
        traces = jnp.maximum(
            0.0, traces + project / (jnp.sum(footprints * footprints, axis=1) + RIDGE)[:, None]
        )
        residual = factor_residual(footprints, traces, sides)
        update = jnp.dot(traces.astype(jnp.bfloat16), residual, preferred_element_type=jnp.float32)
        footprints = jnp.maximum(
            0.0,
            footprints
            + support[None, :] * update / (jnp.sum(traces * traces, axis=1) + RIDGE)[:, None],
        )
    previous = jnp.concatenate([jnp.zeros((comps, 1), jnp.float32), traces[:, :-1]], axis=1)
    spikes = jnp.maximum(0.0, traces - decays[0, 0][:, None] * previous)
    return (
        footprints.astype(jnp.bfloat16).reshape(1, 1, comps, -1),
        traces.reshape(1, 1, comps, VOLUMES),
        spikes.reshape(1, 1, comps, VOLUMES),
    )


def solution(mesh):
    in_specs = (
        P(("parts", "wide"), None, "narrow"),
        P(None, "parts"),
        P(("parts", "wide"), "narrow", None),
        P(("parts", "wide"), "narrow", None),
        P(("parts", "wide"), "narrow", None),
    )
    out_specs = (
        P(("parts", "wide"), "narrow", None, None),
        P(("parts", "wide"), "narrow", None, None),
        P(("parts", "wide"), "narrow", None, None),
    )
    return jax.shard_map(shards, mesh=mesh, in_specs=in_specs, out_specs=out_specs, check_vma=False)
```

profile of v0, /device:TPU:1, one launch (start us, length us, event | category | flops | bytes accessed | tf_op | source)
XLA Modules:
  0.0 822.8 jit_solution(4311231036677110634)
XLA Ops:
  41.0 12.5 %broadcast_in_dim.12 = f32[32,2,128,528]{3,2,1,0:T(8,128)} broadcast(f32[32,128,528]{2,1,0:T(8,128)} %copy.165), dimensions={0,2,3} | broadcast | bytes 25952256 | tf_op jit(solution)/shard_map/broadcast_in_dim | solution.py:94
  53.5 36.6 %reshape.316 = f32[32,135168]{1,0:T(8,128)} reshape(f32[32,2,128,528]{3,2,1,0:T(8,128)} %broadcast_in_dim.12) | data formatting | bytes 34603008 | tf_op jit(solution)/shard_map/reshape | solution.py:94
  105.2 38.7 %while.1 = (s32[]{:T(128)}, bf16[8,520,520]{2,1,0:T(8,128)(2,1)}, s32[8,3]{0,1:T(4,128)S(1)}, bf16[8,512,512]{2,1,0:T(8,128)(2,1)}, s32[]{:T(128)}) while((s32[]{:T(128)}, bf16[8,520,520]{2,1,0:T(8,128)(2,1)}, s32[8,3]{0,1:T(4,128)S(1)}, bf16[8,512,512]{2,1,0:T(8,128)(2,1)}, s32[]{:T(128)}) %tuple.43), condition=%wide.while_cond, body=%wide.while_body.sunk | while | flops 2 | bytes 1050237 | solution.py:37
  178.9 20.4 %dot_general.111 = bf16[2,128,528,32]{2,1,0,3:T(8,128)(2,1)} reshape(bf16[135168,32]{0,1:T(8,128)(2,1)} %convert_bitcast_fusion) | data formatting | bytes 17301504 | tf_op jit(solution)/shard_map/dot_general | solution.py:108
  199.3 15.9 %copy.177 = bf16[2,128,528,32]{1,3,2,0:T(8,128)(2,1)} copy(bf16[2,128,528,32]{2,1,0,3:T(8,128)(2,1)} %dot_general.111) | data formatting | bytes 17301504 | tf_op jit(solution)/shard_map/dot_general | solution.py:108
  224.0 97.5 %all-reduce.15.cloned.1.call-done = f32[2,512,512]{2,1,0:T(8,128)} async-done(((f32[2,512,512]{2,1,0:T(8,128)}), f32[2,512,512]{2,1,0:T(8,128)}) %all-reduce.15.cloned.1.call-update) | async-done | bytes 2097168 | tf_op jit(solution)/shard_map/psum | solution.py:65
  356.0 12.3 %multiply_reduce_fusion.4 = (f32[32]{0:T(128)S(1)}, bf16[32,16]{0,1:T(8,128)(2,1)S(1)}, f32[32,16]{0,1:T(8,128)S(1)}) fusion(f32[32]{0:T(128)S(1)} %broadcast_add_fusion.5, f32[16,2,128,528]{2,0,3,1:T(8,128)} %fusion.69, f32[16,2,128,16]{2,0,3,1:T(8,128)S(1)} %fusion.73, bf16[2,128,528,32]{1,3,2,0:T(8,128)(2,1)} %copy.177, ...), kind=kOutput, calls=%fused_computation.86 | convolution fusion | flops 291965408 | bytes 26217728 | tf_op jit(solution)/shard_map/dot_general | solution.py:135
  396.1 14.0 %reshape.320 = bf16[16,135168]{1,0:T(8,128)(2,1)} reshape(bf16[16,2,128,528]{3,2,1,0:T(8,128)(2,1)} %copy.185) | data formatting | bytes 8650752 | tf_op jit(solution)/shard_map/reshape | solution.py:126
  410.1 15.2 %multiply_reduce_fusion.1 = (f32[32]{0:T(128)S(1)}, bf16[32,135168]{1,0:T(8,128)(2,1)}, f32[32,135168]{1,0:T(8,128)}) fusion(f32[32,135168]{1,0:T(8,128)} %reshape.316, f32[32]{0:T(128)S(1)} %broadcast_add_fusion.4, bf16[32,16]{0,1:T(8,128)(2,1)S(1)} %get-tuple-element.45, bf16[16,135168]{1,0:T(8,128)(2,1)} %reshape.320, f32[135168]{0:T(1024)S(1)} %mul.96), kind=kOutput, calls=%fused_computation.23 | convolution fusion | flops 168689632 | bytes 48121088 | tf_op jit(solution)/shard_map/dot_general | solution.py:145
  425.3 20.9 %reshape.322 = bf16[32,2,128,528]{3,2,1,0:T(8,128)(2,1)} reshape(bf16[32,135168]{1,0:T(8,128)(2,1)} %get-tuple-element.25) | data formatting | bytes 17301504 | tf_op jit(solution)/shard_map/reshape | solution.py:131
  467.0 17.1 %reshape.321 = f32[16,2,128,528]{3,2,1,0:T(8,128)} reshape(f32[16,135168]{1,0:T(8,128)} %fusion.116) | data formatting | bytes 17301504 | tf_op jit(solution)/shard_map/reshape | solution.py:111
  484.0 10.8 %copy.189 = f32[16,2,128,528]{2,0,3,1:T(8,128)} copy(f32[16,2,128,528]{3,2,1,0:T(8,128)} %reshape.321) | data formatting | bytes 17301504 | tf_op jit(solution)/shard_map/reshape | solution.py:111
  514.2 14.1 %reshape.325 = bf16[16,135168]{1,0:T(8,128)(2,1)} reshape(bf16[16,2,128,528]{3,2,1,0:T(8,128)(2,1)} %copy.193) | data formatting | bytes 8650752 | tf_op jit(solution)/shard_map/reshape | solution.py:126
  545.9 17.1 %reshape.326 = f32[16,2,128,528]{3,2,1,0:T(8,128)} reshape(f32[16,135168]{1,0:T(8,128)} %fusion.117) | data formatting | bytes 17301504 | tf_op jit(solution)/shard_map/reshape | solution.py:111
  563.0 10.7 %copy.195 = f32[16,2,128,528]{2,0,3,1:T(8,128)} copy(f32[16,2,128,528]{3,2,1,0:T(8,128)} %reshape.326) | data formatting | bytes 17301504 | tf_op jit(solution)/shard_map/reshape | solution.py:111
  593.2 14.4 %reshape.327 = bf16[16,135168]{1,0:T(8,128)(2,1)} reshape(bf16[16,2,128,528]{3,2,1,0:T(8,128)(2,1)} %copy.197) | data formatting | bytes 8650752 | tf_op jit(solution)/shard_map/reshape | solution.py:126
  607.5 15.2 %multiply_reduce_fusion = (f32[32]{0:T(128)S(1)}, bf16[32,135168]{1,0:T(8,128)(2,1)}, f32[32,135168]{1,0:T(8,128)}) fusion(f32[32,135168]{1,0:T(8,128)} %get-tuple-element.49, f32[32]{0:T(128)S(1)} %broadcast_add_fusion.2, bf16[32,16]{0,1:T(8,128)(2,1)S(1)} %get-tuple-element.43, bf16[16,135168]{1,0:T(8,128)(2,1)} %reshape.327, f32[135168]{0:T(1024)S(1)} %mul.96), kind=kOutput, calls=%fused_computation.22 | convolution fusion | flops 168689632 | bytes 48121088 | tf_op jit(solution)/shard_map/dot_general | solution.py:145
  622.7 20.7 %reshape.329 = bf16[32,2,128,528]{3,2,1,0:T(8,128)(2,1)} reshape(bf16[32,135168]{1,0:T(8,128)(2,1)} %get-tuple-element.23) | data formatting | bytes 17301504 | tf_op jit(solution)/shard_map/reshape | solution.py:131
  662.7 16.8 %reshape.328 = f32[16,2,128,528]{3,2,1,0:T(8,128)} reshape(f32[16,135168]{1,0:T(8,128)} %fusion.118) | data formatting | bytes 17301504 | tf_op jit(solution)/shard_map/reshape | solution.py:111
  679.4 10.8 %copy.201 = f32[16,2,128,528]{2,0,3,1:T(8,128)} copy(f32[16,2,128,528]{3,2,1,0:T(8,128)} %reshape.328) | data formatting | bytes 17301504 | tf_op jit(solution)/shard_map/reshape | solution.py:111
  709.6 14.2 %reshape.332 = bf16[16,135168]{1,0:T(8,128)(2,1)} reshape(bf16[16,2,128,528]{3,2,1,0:T(8,128)(2,1)} %copy.205) | data formatting | bytes 8650752 | tf_op jit(solution)/shard_map/reshape | solution.py:126
  741.9 17.1 %reshape.333 = f32[16,2,128,528]{3,2,1,0:T(8,128)} reshape(f32[16,135168]{1,0:T(8,128)} %fusion.119) | data formatting | bytes 17301504 | tf_op jit(solution)/shard_map/reshape | solution.py:111
  789.1 14.2 %reshape.334 = bf16[16,135168]{1,0:T(8,128)(2,1)} reshape(bf16[16,2,128,528]{3,2,1,0:T(8,128)(2,1)} %copy.209) | data formatting | bytes 8650752 | tf_op jit(solution)/shard_map/reshape | solution.py:126
  803.3 12.1 %fusion.10 = bf16[1,1,32,135168]{3,2,1,0:T(8,128)(2,1)} fusion(f32[32,135168]{1,0:T(8,128)} %get-tuple-element.51, bf16[32,16]{0,1:T(8,128)(2,1)S(1)} %get-tuple-element.41, bf16[16,135168]{1,0:T(8,128)(2,1)} %reshape.334, f32[32]{0:T(128)S(1)} %broadcast_add_fusion, f32[135168]{0:T(1024)S(1)} %mul.96), kind=kOutput, calls=%fused_computation.15 | convolution fusion | flops 160038912 | bytes 30819456 | tf_op jit(solution)/shard_map/dot_general | solution.py:145
  (184 shorter events, 357.0 us)
Async XLA Ops:
  7.2 314.4 %all-reduce.15.cloned.1.call-start = ((), (), s32[]{:S(2)}) async-start(), calls=%async_computation.1 | async-start | bytes 4194304 | tf_op jit(solution)/shard_map/psum | solution.py:65
  7.2 345.6 %collective-permute-start.4 = (bf16[32,16]{0,1:T(8,128)(2,1)S(1)}, bf16[32,16]{0,1:T(8,128)(2,1)S(1)}, u32[]{:S(2)}, u32[]{:S(2)}) collective-permute-start(bf16[32,16]{0,1:T(8,128)(2,1)S(1)} %convert_element_type.154), channel_id=1, source_target_pairs={{0,1},{1,2},{2,3},{4,5},{5,6},{6,7},{8,9},{9,10},{10,11},{12,13},{... | collective-permute-start | bytes 3080 | tf_op jit(solution)/shard_map/ppermute | solution.py:25
  11.7 203.4 %collective-permute-start.6 = (bf16[32,16]{0,1:T(8,128)(2,1)S(1)}, bf16[32,16]{0,1:T(8,128)(2,1)S(1)}, u32[]{:S(2)}, u32[]{:S(2)}) collective-permute-start(bf16[32,16]{0,1:T(8,128)(2,1)S(1)} %convert_element_type.154), channel_id=1, source_target_pairs={{1,0},{2,1},{3,2},{5,4},{6,5},{7,6},{9,8},{10,9},{11,10},{13,12},{... | collective-permute-start | bytes 3080 | tf_op jit(solution)/shard_map/ppermute | solution.py:27
  16.0 79.1 %collective-permute-start.1 = (bf16[8,512,4]{1,0,2:T(8,128)(2,1)S(1)}, bf16[8,512,4]{1,0,2:T(8,128)(2,1)S(1)}, u32[]{:S(2)}, u32[]{:S(2)}) collective-permute-start(bf16[8,512,4]{1,0,2:T(8,128)(2,1)S(1)} %copy.234), channel_id=1, source_target_pairs={{1,0},{2,1},{3,2},{0,3},{5,4},{6,5},{7,6},{4,7},{9,8},{10,9},{11,1... | collective-permute-start | bytes 98312 | tf_op jit(solution)/shard_map/ppermute | solution.py:27
  16.5 73.5 %collective-permute-start = (bf16[8,512,4]{1,0,2:T(8,128)(2,1)S(1)}, bf16[8,512,4]{1,0,2:T(8,128)(2,1)S(1)}, u32[]{:S(2)}, u32[]{:S(2)}) collective-permute-start(bf16[8,512,4]{1,0,2:T(8,128)(2,1)S(1)} %copy.233), channel_id=1, source_target_pairs={{0,1},{1,2},{2,3},{3,0},{4,5},{5,6},{6,7},{7,4},{8,9},{9,10},{10,1... | collective-permute-start | bytes 98312 | tf_op jit(solution)/shard_map/ppermute | solution.py:25
  28.6 186.6 %collective-permute-start.7 = (bf16[32,2,128,16]{2,3,1,0:T(8,128)(2,1)S(1)}, bf16[32,2,128,16]{2,3,1,0:T(8,128)(2,1)S(1)}, u32[]{:S(2)}, u32[]{:S(2)}) collective-permute-start(bf16[32,2,128,16]{2,3,1,0:T(8,128)(2,1)S(1)} %broadcast_in_dim.16), channel_id=1, source_target_pairs={{1,0},{2,1},{3,2},{5,4},{6,5},{7,6},{9,8},{10,9},{11,10},{13,12},{... | collective-permute-start | bytes 786440 | tf_op jit(solution)/shard_map/ppermute | solution.py:27
  90.8 262.1 %collective-permute-start.5 = (bf16[32,2,128,16]{2,3,1,0:T(8,128)(2,1)}, bf16[32,2,128,16]{2,3,1,0:T(8,128)(2,1)S(1)}, u32[]{:S(2)}, u32[]{:S(2)}) collective-permute-start(bf16[32,2,128,16]{2,3,1,0:T(8,128)(2,1)} %broadcast_in_dim.15), channel_id=1, source_target_pairs={{0,1},{1,2},{2,3},{4,5},{5,6},{6,7},{8,9},{9,10},{10,11},{12,13},{... | collective-permute-start | bytes 786440 | tf_op jit(solution)/shard_map/ppermute | solution.py:25
  155.1 15.5 %slice-start.6 = ((s8[8650752]{0:T(1024)(128)(4,1)}), s8[262144]{0:T(1024)(128)(4,1)S(1)}, s32[]{:S(2)}) async-start(s8[8650752]{0:T(1024)(128)(4,1)} %bitcast.190), calls=%async_computation.8 | async-start | bytes 524288
  155.1 167.8 %all-to-all-start = ((bf16[8,512,512]{2,0,1:T(8,128)(2,1)}), bf16[8,512,512]{2,0,1:T(8,128)(2,1)}, u32[]{:S(2)}, u32[]{:S(2)}) async-start(bf16[8,512,512]{2,0,1:T(8,128)(2,1)} %copy.171), calls=%async_computation | async-start | bytes 8388608 | tf_op jit(solution)/shard_map/all_to_all | solution.py:68
  348.5 4.6 collective-permute-start.2
  350.4 5.6 collective-permute-start.3
  356.0 23.8 %copy-start.7 = (bf16[16,2,128,8]{2,0,3,1:T(8,128)(2,1)}, bf16[16,2,128,8]{2,0,3,1:T(8,128)(2,1)S(1)}, u32[]{:S(2)}) copy-start(bf16[16,2,128,8]{2,0,3,1:T(8,128)(2,1)S(1)} %collective-permute-done.3) | copy-start | bytes 196612
  373.3 6.5 collective-permute-start.9
  375.2 4.4 collective-permute-start.8
  452.0 42.8 %collective-permute-start.10 = (bf16[32,2,128,16]{2,3,1,0:T(8,128)(2,1)S(1)}, bf16[32,2,128,16]{2,3,1,0:T(8,128)(2,1)S(1)}, u32[]{:S(2)}, u32[]{:S(2)}) collective-permute-start(bf16[32,2,128,16]{2,3,1,0:T(8,128)(2,1)S(1)} %copy.186), channel_id=1, source_target_pairs={{0,1},{1,2},{2,3},{4,5},{5,6},{6,7},{8,9},{9,10},{10,11},{12,13},{... | collective-permute-start | bytes 786440 | tf_op jit(solution)/shard_map/ppermute | solution.py:25
  465.0 30.0 %collective-permute-start.11 = (bf16[32,2,128,16]{2,3,1,0:T(8,128)(2,1)S(1)}, bf16[32,2,128,16]{2,3,1,0:T(8,128)(2,1)S(1)}, u32[]{:S(2)}, u32[]{:S(2)}) collective-permute-start(bf16[32,2,128,16]{2,3,1,0:T(8,128)(2,1)S(1)} %copy.190), channel_id=1, source_target_pairs={{1,0},{2,1},{3,2},{5,4},{6,5},{7,6},{9,8},{10,9},{11,10},{13,12},{... | collective-permute-start | bytes 786440 | tf_op jit(solution)/shard_map/ppermute | solution.py:27
  514.2 21.3 %slice-start.3 = ((s8[8650752]{0:T(1024)(128)(4,1)}), s8[262144]{0:T(1024)(128)(4,1)S(1)}, s32[]{:S(2)}) async-start(s8[8650752]{0:T(1024)(128)(4,1)} %bitcast.188), calls=%async_computation.5 | async-start | bytes 524288
  540.3 33.6 %collective-permute-start.13 = (bf16[32,16]{0,1:T(8,128)(2,1)S(1)}, bf16[32,16]{0,1:T(8,128)(2,1)S(1)}, u32[]{:S(2)}, u32[]{:S(2)}) collective-permute-start(bf16[32,16]{0,1:T(8,128)(2,1)S(1)} %get-tuple-element.43), channel_id=1, source_target_pairs={{1,0},{2,1},{3,2},{5,4},{6,5},{7,6},{9,8},{10,9},{11,10},{13,12},{... | collective-permute-start | bytes 3080 | tf_op jit(solution)/shard_map/ppermute | solution.py:27
  542.2 31.5 %collective-permute-start.12 = (bf16[32,16]{0,1:T(8,128)(2,1)S(1)}, bf16[32,16]{0,1:T(8,128)(2,1)S(1)}, u32[]{:S(2)}, u32[]{:S(2)}) collective-permute-start(bf16[32,16]{0,1:T(8,128)(2,1)S(1)} %get-tuple-element.43), channel_id=1, source_target_pairs={{0,1},{1,2},{2,3},{4,5},{5,6},{6,7},{8,9},{9,10},{10,11},{12,13},{... | collective-permute-start | bytes 3080 | tf_op jit(solution)/shard_map/ppermute | solution.py:25
  649.4 40.9 %collective-permute-start.14 = (bf16[32,2,128,16]{2,3,1,0:T(8,128)(2,1)S(1)}, bf16[32,2,128,16]{2,3,1,0:T(8,128)(2,1)S(1)}, u32[]{:S(2)}, u32[]{:S(2)}) collective-permute-start(bf16[32,2,128,16]{2,3,1,0:T(8,128)(2,1)S(1)} %copy.198), channel_id=1, source_target_pairs={{0,1},{1,2},{2,3},{4,5},{5,6},{6,7},{8,9},{9,10},{10,11},{12,13},{... | collective-permute-start | bytes 786440 | tf_op jit(solution)/shard_map/ppermute | solution.py:25
  660.7 29.8 %collective-permute-start.15 = (bf16[32,2,128,16]{2,3,1,0:T(8,128)(2,1)S(1)}, bf16[32,2,128,16]{2,3,1,0:T(8,128)(2,1)S(1)}, u32[]{:S(2)}, u32[]{:S(2)}) collective-permute-start(bf16[32,2,128,16]{2,3,1,0:T(8,128)(2,1)S(1)} %copy.202), channel_id=1, source_target_pairs={{1,0},{2,1},{3,2},{5,4},{6,5},{7,6},{9,8},{10,9},{11,10},{13,12},{... | collective-permute-start | bytes 786440 | tf_op jit(solution)/shard_map/ppermute | solution.py:27
  709.6 22.0 %slice-start = ((s8[8650752]{0:T(1024)(128)(4,1)}), s8[262144]{0:T(1024)(128)(4,1)S(1)}, s32[]{:S(2)}) async-start(s8[8650752]{0:T(1024)(128)(4,1)} %bitcast.186), calls=%async_computation.2 | async-start | bytes 524288
  736.4 33.6 %collective-permute-start.17 = (bf16[32,16]{0,1:T(8,128)(2,1)S(1)}, bf16[32,16]{0,1:T(8,128)(2,1)S(1)}, u32[]{:S(2)}, u32[]{:S(2)}) collective-permute-start(bf16[32,16]{0,1:T(8,128)(2,1)S(1)} %get-tuple-element.41), channel_id=1, source_target_pairs={{1,0},{2,1},{3,2},{5,4},{6,5},{7,6},{9,8},{10,9},{11,10},{13,12},{... | collective-permute-start | bytes 3080 | tf_op jit(solution)/shard_map/ppermute | solution.py:27
  738.3 31.5 %collective-permute-start.16 = (bf16[32,16]{0,1:T(8,128)(2,1)S(1)}, bf16[32,16]{0,1:T(8,128)(2,1)S(1)}, u32[]{:S(2)}, u32[]{:S(2)}) collective-permute-start(bf16[32,16]{0,1:T(8,128)(2,1)S(1)} %get-tuple-element.41), channel_id=1, source_target_pairs={{0,1},{1,2},{2,3},{4,5},{5,6},{6,7},{8,9},{9,10},{10,11},{12,13},{... | collective-permute-start | bytes 3080 | tf_op jit(solution)/shard_map/ppermute | solution.py:25
  (15 other events, 119.5 us)
Sparse Core Ops, SparseCore 0:
  155.2 166.3 all-reduce.14
where the time goes:
time: 833 us; the launch traced here: 823 us
  local copies, waits for them, and re-layouts  458 us (55%)
  matrix products  161 us (19%)
  waiting for transfers between devices  101 us (12%)
  starting transfers between devices  51.1 us (6%)
  other arithmetic  35.9 us (4%)
  between operations  15.2 us (2%)
    reshape x8, local copies, waits for them, and re-layouts, factor_residual(): model_ext = model_ext.reshape(VOLUMES, PLANES, rows_patch, ext_width)  111 us
    psum x1, waiting for transfers between devices, shards(): summed = lax.psum(partial_value, 'wide')  97.5 us
    reshape x5, local copies, waits for them, and re-layouts, factor_residual(): return residual.reshape(VOLUMES, -1)  70.8 us
    pad x6, matrix products, factor_residual(): model_ext = model_ext + jnp.pad(part_right, no_pad + ((cols_patch, 0),))  57.4 us
    convert_element_type x5, local copies, waits for them, and re-layouts, factor_residual(): residual = (observed_ext - model_ext).astype(jnp.bfloat16)  44.3 us
    dot_general x3, matrix products, shards(): jnp.dot(traces.astype(jnp.bfloat16), residual, preferred_element_type=jnp...  42.5 us
    reshape x2, local copies, waits for them, and re-layouts, shards(): footprints.astype(jnp.bfloat16)  41.6 us
    gather x24, local copies, waits for them, and re-layouts  38.6 us
  transfers between devices with their start and end apart: 20, of which 3 were waited for; matrix products, arithmetic and copies ran while one was open for 42% of the time, Pallas kernels for 0%

commit v1 on v0

v1 whole, which is shorter than its diff:
```python
import functools

import jax
import jax.numpy as jnp
import numpy as np
from jax import lax
from jax.experimental import pallas as pl
from jax.experimental.pallas import tpu as pltpu
from jax.sharding import PartitionSpec as P

PLANES = 2
VOLUMES = 16
MARGIN = 8
SHIFT_MAX = 4
RADIUS = 12
ITERS = 3
RIDGE = 1.0
EDGE = 2 * MARGIN
LANES = 128
GROUP = 8
VMEM_LIMIT = 48 * 1024 * 1024

f32 = jnp.float32
bf16 = jnp.bfloat16


def roll_lanes(x, shift):
    shift = shift % x.shape[-1]
    return pltpu.roll(x, shift, 1) if shift else x


def lane_iota(shape):
    return lax.broadcasted_iota(jnp.int32, shape, len(shape) - 1)


def pack_kernel(first_ref, last_ref, head_ref, tail_ref):
    frames, height, _ = first_ref.shape
    lane = lane_iota((height, LANES))
    head = jnp.zeros((height, LANES), f32)
    tail = jnp.zeros((height, LANES), f32)
    for f in range(frames):
        here = (lane >= f * EDGE) & (lane < (f + 1) * EDGE)
        head = jnp.where(here, roll_lanes(first_ref[f].astype(f32), f * EDGE), head)
        tail = jnp.where(here, roll_lanes(last_ref[f].astype(f32), (f + 1) * EDGE), tail)
    head_ref[...] = head.astype(bf16)
    tail_ref[...] = tail.astype(bf16)


def pack_edges(recording):
    frames, height, cols = recording.shape
    out = jax.ShapeDtypeStruct((height, LANES), bf16)
    rows = min(height, 128)
    return pl.pallas_call(
        pack_kernel,
        grid=(height // rows,),
        in_specs=[
            pl.BlockSpec((frames, rows, LANES), lambda i: (0, i, 0)),
            pl.BlockSpec((frames, rows, LANES), lambda i: (0, i, cols // LANES - 1)),
        ],
        out_specs=[pl.BlockSpec((rows, LANES), lambda i: (i, 0))] * 2,
        out_shape=[out, out],
        name="pack_edges",
    )(recording, recording)


def register_kernel(shifts_ref, frame_ref, head_ref, tail_ref, core_ref, border_ref, acc_ref):
    f = pl.program_id(0)
    wide, _, rows_patch, cols = core_ref.shape
    height = wide * rows_patch
    width = cols + LANES
    lane = lane_iota((height, LANES))
    back = lax.rem(LANES - f * EDGE, LANES)
    head = pltpu.roll(head_ref[...].astype(f32), back, 1)
    tail = pltpu.roll(tail_ref[...].astype(f32), lax.rem(back + LANES - EDGE, LANES), 1)
    edge = jnp.where(lane < LANES // 2, head, tail)
    frame = jnp.concatenate([frame_ref[0].astype(f32), edge], axis=1)
    row_move = lax.rem(shifts_ref[0, f] + height, height)
    col_move = lax.rem(shifts_ref[1, f] + width, width)
    frame = pltpu.roll(frame, row_move, 0)
    frame = pltpu.roll(frame, col_move, 1)
    core_ref[...] = frame[:, :cols].astype(bf16).reshape(wide, 1, rows_patch, cols)
    moved = pltpu.roll(frame[:, cols:], lax.rem(f * EDGE + MARGIN, LANES), 1)
    here = (lane >= f * EDGE) & (lane < (f + 1) * EDGE)

    @pl.when(f == 0)
    def _():
        acc_ref[...] = jnp.zeros_like(acc_ref)

    acc_ref[...] = jnp.where(here, moved, acc_ref[...])

    @pl.when(f == pl.num_programs(0) - 1)
    def _():
        border_ref[...] = acc_ref[...].astype(bf16).reshape(border_ref.shape)


def register(shifts, recording, head, tail, wide):
    frames, height, cols = recording.shape
    rows_patch = height // wide
    whole = pl.BlockSpec((height, LANES), lambda f: (0, 0))
    return pl.pallas_call(
        register_kernel,
        grid=(frames,),
        in_specs=[
            pl.BlockSpec(memory_space=pltpu.SMEM),
            pl.BlockSpec((1, height, cols), lambda f: (f, 0, 0)),
            whole,
            whole,
        ],
        out_specs=[
            pl.BlockSpec((wide, 1, rows_patch, cols), lambda f: (0, f, 0, 0)),
            pl.BlockSpec((wide, rows_patch, LANES), lambda f: (0, 0, 0)),
        ],
        out_shape=[
            jax.ShapeDtypeStruct((wide, frames, rows_patch, cols), bf16),
            jax.ShapeDtypeStruct((wide, rows_patch, LANES), bf16),
        ],
        scratch_shapes=[pltpu.VMEM((height, LANES), f32)],
        compiler_params=pltpu.CompilerParams(vmem_limit_bytes=VMEM_LIMIT),
        name="register",
    )(shifts, recording, head, tail)


def bump(position, center):
    return jnp.maximum(0.0, 1.0 - jnp.abs(position - center) * (1.0 / RADIUS))


def lane_pieces(cols):
    return [(j * cols, cols if j < GROUP else LANES) for j in range(GROUP + 1)]


NT = (((1,), (1,)), ((), ()))


def nt_dot(a, b):
    return lax.dot_general(a, b, NT, preferred_element_type=f32)


def observe_kernel(
    mix_ref, recv_ref, border_ref, pattern_ref, centers_ref, obs_ref, traces_ref, proj_ref, energy_ref
):
    volumes, rows, cols = recv_ref.shape
    sources = border_ref.shape[0]
    per_source = volumes // sources
    step = pl.program_id(0) * pl.num_programs(1) + pl.program_id(1)
    last = pl.num_programs(0) * pl.num_programs(1) - 1
    base = (pl.program_id(1) * rows).astype(f32)
    mix = mix_ref[...]

    @pl.when(step == 0)
    def _():
        proj_ref[...] = jnp.zeros_like(proj_ref)
        energy_ref[...] = jnp.zeros_like(energy_ref)

    core = jnp.dot(mix, recv_ref[...].reshape(volumes * rows, cols), preferred_element_type=f32)
    strips = [border_ref[s].astype(f32) for s in range(sources)]
    border = jnp.concatenate(
        [
            roll_lanes(strips[v // per_source], -(v % per_source) * EDGE - MARGIN)
            for v in range(volumes)
        ],
        axis=0,
    ).astype(bf16)
    border = jnp.dot(mix, border, preferred_element_type=f32)
    lane = lane_iota((volumes, LANES))
    center_row = centers_ref[:, 0:1]
    center_col = centers_ref[:, 1:2]
    size = GROUP * (cols + EDGE)
    proj = proj_ref[...]
    energy = energy_ref[...]
    for g in range(rows // GROUP):
        carry = None
        for j, (start, width) in enumerate(lane_pieces(cols)):
            if j < GROUP:
                at = (g * GROUP + j) * volumes
                line = jnp.concatenate(
                    [core[at : at + volumes], border[at : at + volumes]], axis=1
                )
                line = roll_lanes(line, MARGIN + EDGE * j)
                first = line[:, :LANES]
                if carry is not None:
                    first = jnp.where(lane < EDGE * j, carry, first)
                carry = line[:, cols:]
                piece = jnp.concatenate([first, line[:, LANES:cols]], axis=1)
            else:
                piece = carry
            low = piece.astype(bf16)
            obs_ref[:, g * size + start : g * size + start + width] = low
            row = pattern_ref[0:1, start : start + width] + (base + g * GROUP)
            col = pattern_ref[1:2, start : start + width]
            inside = pattern_ref[2:3, start : start + width]
            foot = bump(row, center_row) * (bump(col, center_col) * inside)
            proj = proj + nt_dot(foot.astype(bf16), low)
            square = foot * foot
            for c in range(width // LANES):
                energy = energy + square[:, c * LANES : (c + 1) * LANES]
    proj_ref[...] = proj
    energy_ref[...] = energy

    @pl.when(step == last)
    def _():
        total = jnp.sum(energy, axis=1, keepdims=True) + RIDGE
        traces_ref[...] = jnp.maximum(0.0, proj / total)


def observe(received, border, pattern, centers, frames):
    _, rows_patch, cols = received.shape
    comps = centers.shape[0]
    rows = 16
    blocks = rows_patch // rows
    sources = border.shape[0] // PLANES
    size = GROUP * (cols + EDGE)
    same = np.eye(rows)
    mix = np.einsum("yx,vu->yvux", same, np.eye(VOLUMES) - 1.0 / VOLUMES)
    mix = jnp.asarray(mix.reshape(rows * VOLUMES, VOLUMES * rows), bf16)
    flat = PLANES * rows_patch * (cols + EDGE)
    return pl.pallas_call(
        observe_kernel,
        grid=(PLANES, blocks),
        in_specs=[
            pl.BlockSpec(mix.shape, lambda p, y: (0, 0)),
            pl.BlockSpec((VOLUMES, rows, cols), lambda p, y: (p, y, 0)),
            pl.BlockSpec((sources, rows, LANES), lambda p, y: (p, y, 0)),
            pl.BlockSpec((8, size), lambda p, y: (0, 0)),
            pl.BlockSpec((comps, LANES), lambda p, y: (0, 0)),
        ],
        out_specs=[
            pl.BlockSpec((VOLUMES, rows * (cols + EDGE)), lambda p, y: (0, p * blocks + y)),
            pl.BlockSpec((comps, VOLUMES), lambda p, y: (0, 0)),
        ],
        out_shape=[
            jax.ShapeDtypeStruct((VOLUMES, flat), bf16),
            jax.ShapeDtypeStruct((comps, VOLUMES), f32),
        ],
        scratch_shapes=[pltpu.VMEM((comps, VOLUMES), f32), pltpu.VMEM((comps, LANES), f32)],
        compiler_params=pltpu.CompilerParams(vmem_limit_bytes=VMEM_LIMIT),
        name="observe",
    )(mix, received, border, pattern, centers)


def sweep_kernel(rows_patch, cols, first, final, *refs):
    traces_ref, left_ref, right_ref, pattern_ref, centers_ref, obs_ref = refs[:6]
    refs = refs[6:]
    if not first:
        foot_ref, side_ref = refs[:2]
        refs = refs[2:]
    if final:
        (low_ref,) = refs
    else:
        new_foot_ref, new_side_ref, new_traces_ref, proj_ref, energy_ref = refs
    size = GROUP * (cols + EDGE)
    side_size = (GROUP + 1) * LANES
    groups = obs_ref.shape[1] // size
    volumes = obs_ref.shape[0]
    comps = traces_ref.shape[0]
    step = pl.program_id(0)

    eye_at = lax.broadcasted_iota(jnp.int32, (volumes, volumes), 0)
    eye = (eye_at == lax.broadcasted_iota(jnp.int32, (volumes, volumes), 1)).astype(f32).astype(bf16)

    def prepared(ref):
        full = ref[...]
        low = full.astype(bf16)
        flipped = nt_dot(eye, low).astype(bf16)
        scale = 1.0 / (jnp.sum(full * full, axis=1, keepdims=True) + RIDGE)
        return low, flipped, scale

    own, own_t, own_scale = prepared(traces_ref)
    left, left_t, left_scale = prepared(left_ref)
    right, right_t, right_scale = prepared(right_ref)

    if not final:

        @pl.when(step == 0)
        def _():
            proj_ref[...] = jnp.zeros_like(proj_ref)
            energy_ref[...] = jnp.zeros_like(energy_ref)

    def one_group(g, _):
        at = pl.multiple_of(g * size, LANES)
        side_at = pl.multiple_of(g * side_size, LANES)
        base = lax.rem((step * groups + g) * GROUP, rows_patch).astype(f32)
        if not final:
            proj = proj_ref[...]
            energy = energy_ref[...]
        for j, (start, width) in enumerate(lane_pieces(cols)):
            where = pl.ds(at + start, width)
            side_where = pl.ds(side_at + j * LANES, LANES)
            inside = pattern_ref[2:3, start : start + width]
            is_left = pattern_ref[3:4, start : start + LANES]
            is_right = pattern_ref[4:5, start : start + LANES]
            obs = obs_ref[:, where].astype(f32)
            if first:
                row = pattern_ref[0:1, start : start + width] + base
                col = pattern_ref[1:2, start : start + width]
                foot = bump(row, centers_ref[:, 0:1]) * (bump(col, centers_ref[:, 1:2]) * inside)
                row, col = row[:, :LANES], col[:, :LANES]
                side = bump(row, centers_ref[:, 2:3]) * (
                    bump(col + cols, centers_ref[:, 3:4]) * is_left
                ) + bump(row, centers_ref[:, 4:5]) * (
                    bump(col - cols, centers_ref[:, 5:6]) * is_right
                )
            else:
                foot = foot_ref[:, where]
                side = side_ref[:, side_where]

            def residual(foot_low, side):
                model = jnp.dot(own_t, foot_low, preferred_element_type=f32)
                extra = jnp.dot(left_t, (side * is_left).astype(bf16), preferred_element_type=f32)
                extra = extra + jnp.dot(
                    right_t, (side * is_right).astype(bf16), preferred_element_type=f32
                )
                head = model[:, :LANES] + extra
                model = head if width == LANES else jnp.concatenate([head, model[:, LANES:]], axis=1)
                return (obs - model).astype(bf16)

            rest = residual(foot.astype(bf16), side)
            update = jnp.dot(own, rest, preferred_element_type=f32)
            foot = jnp.maximum(0.0, foot + inside * (update * own_scale))
            foot_low = foot.astype(bf16)
            if final:
                low_ref[:, where] = foot_low
                continue
            update_left = jnp.dot(left, rest[:, :LANES], preferred_element_type=f32)
            update_right = jnp.dot(right, rest[:, :LANES], preferred_element_type=f32)
            side = jnp.maximum(
                0.0,
                side
                + is_left * (update_left * left_scale)
                + is_right * (update_right * right_scale),
            )
            new_foot_ref[:, where] = foot
            new_side_ref[:, side_where] = side
            proj = proj + nt_dot(foot_low, residual(foot_low, side))
            square = foot * foot
            for c in range(width // LANES):
                energy = energy + square[:, c * LANES : (c + 1) * LANES]
        if not final:
            proj_ref[...] = proj
            energy_ref[...] = energy
        return 0

    lax.fori_loop(0, groups, one_group, 0)

    if not final:

        @pl.when(step == pl.num_programs(0) - 1)
        def _():
            total = jnp.sum(energy_ref[...], axis=1, keepdims=True) + RIDGE
            new_traces_ref[...] = jnp.maximum(0.0, traces_ref[...] + proj_ref[...] / total)


def sweep(traces, left, right, pattern, centers, observed, state, rows_patch, cols, final):
    comps, volumes = traces.shape
    flat = observed.shape[1]
    groups_all = flat // (GROUP * (cols + EDGE))
    per_block = 4
    blocks = groups_all // per_block
    size = per_block * GROUP * (cols + EDGE)
    side_size = per_block * (GROUP + 1) * LANES
    small = pl.BlockSpec((comps, volumes), lambda i: (0, 0))
    foot_spec = pl.BlockSpec((comps, size), lambda i: (0, i))
    side_spec = pl.BlockSpec((comps, side_size), lambda i: (0, i))
    first = state is None
    in_specs = [
        small,
        small,
        small,
        pl.BlockSpec(pattern.shape, lambda i: (0, 0)),
        pl.BlockSpec(centers.shape, lambda i: (0, 0)),
        pl.BlockSpec((volumes, size), lambda i: (0, i)),
    ]
    args = [traces, left, right, pattern, centers, observed]
    if not first:
        in_specs += [foot_spec, side_spec]
        args += list(state)
    if final:
        out_specs = [foot_spec]
        out_shape = [jax.ShapeDtypeStruct((comps, flat), bf16)]
        scratch = []
    else:
        out_specs = [foot_spec, side_spec, small]
        out_shape = [
            jax.ShapeDtypeStruct((comps, flat), f32),
            jax.ShapeDtypeStruct((comps, blocks * side_size), f32),
            jax.ShapeDtypeStruct((comps, volumes), f32),
        ]
        scratch = [pltpu.VMEM((comps, volumes), f32), pltpu.VMEM((comps, LANES), f32)]
    return pl.pallas_call(
        functools.partial(sweep_kernel, rows_patch, cols, first, final),
        grid=(blocks,),
        in_specs=in_specs,
        out_specs=out_specs,
        out_shape=out_shape,
        scratch_shapes=scratch,
        compiler_params=pltpu.CompilerParams(vmem_limit_bytes=VMEM_LIMIT),
        name="sweep",
    )(*args)


def from_neighbours(value, axis):
    count = lax.axis_size(axis)
    left = lax.ppermute(value, axis, [(i, i + 1) for i in range(count - 1)])
    right = lax.ppermute(value, axis, [(i + 1, i) for i in range(count - 1)])
    return left, right


def shards(recording, offsets, center_rows, center_cols, decays):
    frames_dev, height, cols = recording.shape
    wide = lax.axis_size("wide")
    narrow = lax.axis_size("narrow")
    rows_patch = height // wide
    ext_width = cols + EDGE
    comps = center_rows.shape[-1]

    head, tail = pack_edges(recording)
    ring = [(i, (i + 1) % narrow) for i in range(narrow)]
    tail = lax.ppermute(tail, "narrow", ring)
    head = lax.ppermute(head, "narrow", [(b, a) for a, b in ring])
    shifts = lax.dynamic_slice_in_dim(offsets, lax.axis_index("wide") * frames_dev, frames_dev, 1)
    core, border = register(shifts, recording, head, tail, wide)
    received = lax.all_to_all(core, "wide", split_axis=0, concat_axis=0, tiled=True)
    border = lax.all_to_all(border, "wide", split_axis=0, concat_axis=0, tiled=True)
    received = received.reshape(wide * frames_dev, rows_patch, cols)

    place = np.arange(GROUP * ext_width)
    row = place // ext_width
    col = place % ext_width - MARGIN
    global_col = lax.axis_index("narrow") * cols + jnp.asarray(col, jnp.int32)
    inside = ((global_col >= 0) & (global_col < cols * narrow)).astype(f32)
    is_left = jnp.asarray(col < MARGIN, f32) * inside
    is_right = jnp.asarray(col >= cols - MARGIN, f32) * inside
    zero = jnp.zeros_like(inside)
    pattern = jnp.stack(
        [jnp.asarray(row, f32), jnp.asarray(col, f32), inside, is_left, is_right, zero, zero, zero]
    )
    centers = jnp.stack([center_rows[0, 0], center_cols[0, 0]], axis=1).astype(f32)
    left, right = from_neighbours(centers, "narrow")
    centers = jnp.concatenate(
        [centers, left, right, jnp.zeros((comps, LANES - 6), f32)], axis=1
    )

    observed, traces = observe(received, border, pattern, centers, frames_dev)
    state = None
    for turn in range(ITERS):
        left, right = from_neighbours(traces, "narrow")
        final = turn == ITERS - 1
        out = sweep(
            traces, left, right, pattern, centers, observed, state, rows_patch, cols, final
        )
        if final:
            footprints = out[0]
        else:
            state, traces = out[:2], out[2]
    previous = jnp.concatenate([jnp.zeros((comps, 1), f32), traces[:, :-1]], axis=1)
    spikes = jnp.maximum(0.0, traces - decays[0, 0][:, None] * previous)
    return (
        footprints.reshape(1, 1, comps, -1),
        traces.reshape(1, 1, comps, VOLUMES),
        spikes.reshape(1, 1, comps, VOLUMES),
    )


def solution(mesh):
    in_specs = (
        P(("parts", "wide"), None, "narrow"),
        P(None, "parts"),
        P(("parts", "wide"), "narrow", None),
        P(("parts", "wide"), "narrow", None),
        P(("parts", "wide"), "narrow", None),
    )
    out_specs = (
        P(("parts", "wide"), "narrow", None, None),
        P(("parts", "wide"), "narrow", None, None),
        P(("parts", "wide"), "narrow", None, None),
    )
    return jax.shard_map(shards, mesh=mesh, in_specs=in_specs, out_specs=out_specs, check_vma=False)
```

time: 833 us -> 417 us (0.50); the launches traced: 823 us -> 416 us
  local copies, waits for them, and re-layouts: 458 us -> 8.34 us
  Pallas kernels: 0 us -> 273 us
  matrix products: 161 us -> 0 us
  other arithmetic: 35.9 us -> 0.19 us
  starting transfers between devices: 51.1 us -> 34.7 us
  between operations: 15.2 us -> 0.94 us
  waiting for transfers between devices: 101 us -> 89.4 us
  blocking collectives: 0 us -> 9.3 us
    pallas_call x0 -> x6, Pallas kernels: none -> 273 us  [the longest x3 243 us: sweep(): pl.pallas_call(functools.partial(sweep_kernel, rows_patch, cols, first, f...]
    reshape x16 -> x0, local copies, waits for them, and re-layouts: 260 us -> none  [the longest x8 111 us: factor_residual(): model_ext = model_ext.reshape(VOLUMES, PLANES, rows_patch, ext_width)]
    dot_general x18 -> x0, matrix products: 104 us -> none  [the longest x3 42.5 us: shards(): jnp.dot(traces.astype(jnp.bfloat16), residual, preferred_element_type=jnp...]
    psum x1 -> x0, waiting for transfers between devices: 97.5 us -> none  [shards(): summed = lax.psum(partial_value, 'wide')]
    all_to_all x1, waiting for transfers between devices: 0.01 us -> 83.8 us  [shards(): lax.all_to_all(core, 'wide', split_axis=0, concat_axis=0, tiled=True)]
    convert_element_type x9 -> x0, local copies, waits for them, and re-layouts: 64.3 us -> none  [the longest x5 44.3 us: factor_residual(): residual = (observed_ext - model_ext).astype(jnp.bfloat16)]
    pad x6 -> x0, matrix products: 57.4 us -> none  [factor_residual(): model_ext = model_ext + jnp.pad(part_right, no_pad + ((cols_patch, 0),))]
    gather x25 -> x0, local copies, waits for them, and re-layouts: 45.3 us -> none
  transfers between devices with their start and end apart: 20 -> 11, of which waited for: 3 -> 5; matrix products, arithmetic and copies ran while one was open for 42% -> 0% of each run, Pallas kernels for 0% -> 0%
where the time goes in v1:
time: 417 us; the launch traced here: 416 us
  Pallas kernels  273 us (65%)
  waiting for transfers between devices  89.4 us (21%)
  starting transfers between devices  34.7 us (8%)
  blocking collectives  9.3 us (2%)
  local copies, waits for them, and re-layouts  8.34 us (2%)
    pallas_call x3, Pallas kernels, sweep(): pl.pallas_call(functools.partial(sweep_kernel, rows_patch, cols, first, f...  243 us
    all_to_all x1, waiting for transfers between devices, shards(): lax.all_to_all(core, 'wide', split_axis=0, concat_axis=0, tiled=True)  83.8 us
    pallas_call x1, Pallas kernels, observe(): pl.pallas_call(observe_kernel, grid=(PLANES, blocks), in_specs=[pl.BlockS...  17.1 us
    ppermute x4, starting transfers between devices, from_neighbours(): left = lax.ppermute(value, axis, [(i, i + 1) for i in range(count - 1)])  15.5 us
    ppermute x4, starting transfers between devices, from_neighbours(): right = lax.ppermute(value, axis, [(i + 1, i) for i in range(count - 1)])  11.8 us
    pallas_call x1, Pallas kernels, register(): pl.pallas_call(register_kernel, grid=(frames,), in_specs=[pl.BlockSpec(me...  9.52 us
    all_to_all x1, blocking collectives, shards(): lax.all_to_all(border, 'wide', split_axis=0, concat_axis=0, tiled=True)  9.3 us
  transfers between devices with their start and end apart: 11, of which 5 were waited for; matrix products, arithmetic and copies ran while one was open for 0% of the time, Pallas kernels for 0%

profile of v1, /device:TPU:1, one launch (start us, length us, event | category | flops | bytes accessed | tf_op | source)
XLA Modules:
  0.0 415.9 jit_solution(10820513877832278847)
XLA Ops:
  0.6 3.8 pack_edges.1
  4.5 2.6 collective-permute-start.1
  7.2 3.6 collective-permute-done.head_ref
  10.7 9.5 %register.1 = (bf16[4,8,128,512]{3,2,1,0:T(8,128)(2,1)S(1)}, bf16[4,128,128]{2,1,0:T(8,128)(2,1)S(1)}) custom-call(s32[2,8]{1,0:T(2,128)S(1)} %constant_dynamic-slice_fusion.shifts_ref, bf16[8,512,512]{2,1,0:T(8,128)(2,1)} %frame_ref.1, bf16[512,128]{1,0:T(8,128)(2,1)S(1)} %collective-permute-done.head_ref, bf16[512,128]{1,0:T(8,128)(2,1)S(1)} %collective-permute-done.1.tail_ref), custom_call_target="tpu_custom_call" | custom-call | tf_op jit(solution)/shard_map/register/pallas_call | solution.py:100
  20.3 2.0 copy-done.4
  22.3 9.3 %all_to_all.10.border_ref = bf16[4,128,128]{2,1,0:T(8,128)(2,1)S(1)} all-to-all(bf16[4,128,128]{2,1,0:T(8,128)(2,1)S(1)} %get-tuple-element.18), channel_id=1, replica_groups=mesh['parts'=2,'wide'=4,'narrow'=4] {'wide'}, dimensions={0} | all-to-all | bytes 262144 | tf_op jit(solution)/shard_map/all_to_all | solution.py:422
  31.6 4.9 %all-to-all-start = ((bf16[4,8,128,512]{3,2,1,0:T(8,128)(2,1)}), bf16[4,8,128,512]{3,2,1,0:T(8,128)(2,1)}, u32[]{:S(2)}, u32[]{:S(2)}) async-start(bf16[4,8,128,512]{3,2,1,0:T(8,128)(2,1)} %copy-done.4), calls=%async_computation | async-start | bytes 8388608 | tf_op jit(solution)/shard_map/all_to_all | solution.py:421
  36.6 4.6 %collective-permute-start.3 = (f32[32,2]{1,0:T(8,128)S(1)}, f32[32,2]{1,0:T(8,128)S(1)}, u32[]{:S(2)}, u32[]{:S(2)}) collective-permute-start(f32[32,2]{1,0:T(8,128)S(1)} %convert_element_type.4), channel_id=1, source_target_pairs={{1,0},{2,1},{3,2},{5,4},{6,5},{7,6},{9,8},{10,9},{11,10},{13,12},{... | collective-permute-start | bytes 776 | tf_op jit(solution)/shard_map/ppermute | solution.py:403
  41.2 3.2 collective-permute-start.2
  45.4 83.8 %all-to-all-done = bf16[4,8,128,512]{3,2,1,0:T(8,128)(2,1)} async-done(((bf16[4,8,128,512]{3,2,1,0:T(8,128)(2,1)}), bf16[4,8,128,512]{3,2,1,0:T(8,128)(2,1)}, u32[]{:S(2)}, u32[]{:S(2)}) %all-to-all-start) | async-done | bytes 4194336 | tf_op jit(solution)/shard_map/all_to_all | solution.py:421
  129.2 17.1 %observe.1 = (bf16[16,135168]{1,0:T(8,128)(2,1)}, f32[32,16]{1,0:T(8,128)S(1)}) custom-call(bf16[256,256]{1,0:T(8,128)(2,1)S(1)} %copy-done.5, bf16[32,128,512]{2,1,0:T(8,128)(2,1)} %bitcast.recv_ref, bf16[4,128,128]{2,1,0:T(8,128)(2,1)S(1)} %all_to_all.10.border_ref, f32[8,4224]{1,0:T(8,128)S(1)} %stack.34.pattern_ref.refs_3_, ...), custom_call_target="tpu_custom_call" | custom-call | tf_op jit(solution)/shard_map/observe/pallas_call | solution.py:216
  146.3 3.4 collective-permute-start.5
  149.7 3.8 collective-permute-start.4
  153.5 0.8 collective-permute-done.4.refs_1_
  154.4 2.2 copy-done.2
  156.6 98.8 %sweep.3 = (f32[32,135168]{1,0:T(8,128)}, f32[32,36864]{1,0:T(8,128)}, f32[32,16]{1,0:T(8,128)S(1)}) custom-call(f32[32,16]{1,0:T(8,128)S(1)} %get-tuple-element.19.refs_0_, f32[32,16]{1,0:T(8,128)S(1)} %collective-permute-done.4.refs_1_, f32[32,16]{1,0:T(8,128)S(1)} %collective-permute-done.5.refs_2_, f32[8,4224]{1,0:T(8,128)S(1)} %stack.34.pattern_ref.refs_3_, ...), custom_call_target="tpu_custom_call" | custom-call | tf_op jit(solution)/shard_map/sweep/pallas_call | solution.py:388
  255.4 1.9 collective-permute-start.7
  257.3 4.2 %collective-permute-start.6 = (f32[32,16]{1,0:T(8,128)S(1)}, f32[32,16]{1,0:T(8,128)S(1)}, u32[]{:S(2)}, u32[]{:S(2)}) collective-permute-start(f32[32,16]{1,0:T(8,128)S(1)} %get-tuple-element.21.refs_0_), channel_id=1, source_target_pairs={{0,1},{1,2},{2,3},{4,5},{5,6},{6,7},{8,9},{9,10},{10,11},{12,13},{... | collective-permute-start | bytes 6152 | tf_op jit(solution)/shard_map/ppermute | solution.py:402
  261.5 0.8 collective-permute-done.6.refs_1_
  262.4 96.2 %sweep.4 = (f32[32,135168]{1,0:T(8,128)}, f32[32,36864]{1,0:T(8,128)}, f32[32,16]{1,0:T(8,128)S(1)}) custom-call(f32[32,16]{1,0:T(8,128)S(1)} %get-tuple-element.21.refs_0_, f32[32,16]{1,0:T(8,128)S(1)} %collective-permute-done.6.refs_1_, f32[32,16]{1,0:T(8,128)S(1)} %collective-permute-done.7.refs_2_, f32[8,4224]{1,0:T(8,128)S(1)} %stack.34.pattern_ref.refs_3_, ...), custom_call_target="tpu_custom_call" | custom-call | tf_op jit(solution)/shard_map/sweep/pallas_call | solution.py:388
  358.6 1.9 collective-permute-start.9
  360.5 4.2 %collective-permute-start.8 = (f32[32,16]{1,0:T(8,128)S(1)}, f32[32,16]{1,0:T(8,128)S(1)}, u32[]{:S(2)}, u32[]{:S(2)}) collective-permute-start(f32[32,16]{1,0:T(8,128)S(1)} %get-tuple-element.24.refs_0_), channel_id=1, source_target_pairs={{0,1},{1,2},{2,3},{4,5},{5,6},{6,7},{8,9},{9,10},{10,11},{12,13},{... | collective-permute-start | bytes 6152 | tf_op jit(solution)/shard_map/ppermute | solution.py:402
  366.1 2.2 copy-done.3
  368.3 47.6 %sweep.5 = bf16[32,135168]{1,0:T(8,128)(2,1)} custom-call(f32[32,16]{1,0:T(8,128)S(1)} %get-tuple-element.24.refs_0_, f32[32,16]{1,0:T(8,128)S(1)} %collective-permute-done.8.refs_1_, f32[32,16]{1,0:T(8,128)S(1)} %collective-permute-done.9.refs_2_, f32[8,4224]{1,0:T(8,128)S(1)} %stack.34.pattern_ref.refs_3_, ...), custom_call_target="tpu_custom_call" | custom-call | tf_op jit(solution)/shard_map/sweep/pallas_call | solution.py:388
  (51 shorter events, 2.5 us)
Async XLA Ops:
  0.6 6.5 %copy-start = (s32[2,32]{1,0:T(2,128)S(1)}, s32[2,32]{1,0:T(2,128)}, u32[]{:S(2)}) copy-start(s32[2,32]{1,0:T(2,128)} %param.12) | copy-start | bytes 772
  4.4 6.3 %collective-permute-start = (bf16[512,128]{1,0:T(8,128)(2,1)}, bf16[512,128]{1,0:T(8,128)(2,1)S(1)}, u32[]{:S(2)}, u32[]{:S(2)}) collective-permute-start(bf16[512,128]{1,0:T(8,128)(2,1)} %get-tuple-element.15), channel_id=1, source_target_pairs={{1,0},{2,1},{3,2},{0,3},{5,4},{6,5},{7,6},{4,7},{9,8},{10,9},{11,1... | collective-permute-start | bytes 393224 | tf_op jit(solution)/shard_map/ppermute | solution.py:418
  4.5 6.2 %collective-permute-start.1 = (bf16[512,128]{1,0:T(8,128)(2,1)}, bf16[512,128]{1,0:T(8,128)(2,1)S(1)}, u32[]{:S(2)}, u32[]{:S(2)}) collective-permute-start(bf16[512,128]{1,0:T(8,128)(2,1)} %get-tuple-element.16), channel_id=1, source_target_pairs={{0,1},{1,2},{2,3},{3,0},{4,5},{5,6},{6,7},{7,4},{8,9},{9,10},{10,1... | collective-permute-start | bytes 393224 | tf_op jit(solution)/shard_map/ppermute | solution.py:417
  22.3 14.2 %copy-start.12 = (s32[1,1,32]{2,1,0:T(1,128)S(1)}, s32[1,1,32]{2,1,0:T(1,128)}, u32[]{:S(2)}) copy-start(s32[1,1,32]{2,1,0:T(1,128)} %param.14) | copy-start | bytes 388
  22.3 14.2 %copy-start.13 = (s32[1,1,32]{2,1,0:T(1,128)S(1)}, s32[1,1,32]{2,1,0:T(1,128)}, u32[]{:S(2)}) copy-start(s32[1,1,32]{2,1,0:T(1,128)} %param.13) | copy-start | bytes 388
  22.3 22.2 %copy-start.6 = (s32[4224]{0:T(1024)S(1)}, s32[4224]{0:T(1024)}, u32[]{:S(2)}) copy-start(s32[4224]{0:T(1024)} %constant.38.clone) | copy-start | bytes 50692
  22.3 22.2 %copy-start.7 = (f32[4224]{0:T(1024)S(1)}, f32[4224]{0:T(1024)}, u32[]{:S(2)}) copy-start(f32[4224]{0:T(1024)} %constant.40.clone) | copy-start | bytes 50692
  22.3 22.2 %copy-start.8 = (f32[4224]{0:T(1024)S(1)}, f32[4224]{0:T(1024)}, u32[]{:S(2)}) copy-start(f32[4224]{0:T(1024)} %constant.39.clone) | copy-start | bytes 50692
  22.3 22.4 %copy-start.9 = (f32[1,4224]{1,0:T(1,128)S(1)}, f32[1,4224]{1,0:T(1,128)}, u32[]{:S(2)}) copy-start(f32[1,4224]{1,0:T(1,128)} %constant.50) | copy-start | bytes 50692
  22.3 22.4 %copy-start.10 = (f32[1,4224]{1,0:T(1,128)S(1)}, f32[1,4224]{1,0:T(1,128)}, u32[]{:S(2)}) copy-start(f32[1,4224]{1,0:T(1,128)} %constant.49) | copy-start | bytes 50692
  22.3 106.9 %copy-start.5 = (bf16[256,256]{1,0:T(8,128)(2,1)S(1)}, bf16[256,256]{1,0:T(8,128)(2,1)}, u32[]{:S(2)}) copy-start(bf16[256,256]{1,0:T(8,128)(2,1)} %constant.43.clone.mix_ref) | copy-start | bytes 393220
  31.6 97.5 %all-to-all-start = ((bf16[4,8,128,512]{3,2,1,0:T(8,128)(2,1)}), bf16[4,8,128,512]{3,2,1,0:T(8,128)(2,1)}, u32[]{:S(2)}, u32[]{:S(2)}) async-start(bf16[4,8,128,512]{3,2,1,0:T(8,128)(2,1)} %copy-done.4), calls=%async_computation | async-start | bytes 8388608 | tf_op jit(solution)/shard_map/all_to_all | solution.py:421
  36.6 8.3 %collective-permute-start.3 = (f32[32,2]{1,0:T(8,128)S(1)}, f32[32,2]{1,0:T(8,128)S(1)}, u32[]{:S(2)}, u32[]{:S(2)}) collective-permute-start(f32[32,2]{1,0:T(8,128)S(1)} %convert_element_type.4), channel_id=1, source_target_pairs={{1,0},{2,1},{3,2},{5,4},{6,5},{7,6},{9,8},{10,9},{11,10},{13,12},{... | collective-permute-start | bytes 776 | tf_op jit(solution)/shard_map/ppermute | solution.py:403
  41.2 4.1 collective-permute-start.2
  146.3 7.2 %collective-permute-start.5 = (f32[32,16]{1,0:T(8,128)S(1)}, f32[32,16]{1,0:T(8,128)S(1)}, u32[]{:S(2)}, u32[]{:S(2)}) collective-permute-start(f32[32,16]{1,0:T(8,128)S(1)} %get-tuple-element.19.refs_0_), channel_id=1, source_target_pairs={{1,0},{2,1},{3,2},{5,4},{6,5},{7,6},{9,8},{10,9},{11,10},{13,12},{... | collective-permute-start | bytes 6152 | tf_op jit(solution)/shard_map/ppermute | solution.py:403
  149.7 4.7 %collective-permute-start.4 = (f32[32,16]{1,0:T(8,128)S(1)}, f32[32,16]{1,0:T(8,128)S(1)}, u32[]{:S(2)}, u32[]{:S(2)}) collective-permute-start(f32[32,16]{1,0:T(8,128)S(1)} %get-tuple-element.19.refs_0_), channel_id=1, source_target_pairs={{0,1},{1,2},{2,3},{4,5},{5,6},{6,7},{8,9},{9,10},{10,11},{12,13},{... | collective-permute-start | bytes 6152 | tf_op jit(solution)/shard_map/ppermute | solution.py:402
  154.4 2.2 copy-start.2
  255.4 6.1 %collective-permute-start.7 = (f32[32,16]{1,0:T(8,128)S(1)}, f32[32,16]{1,0:T(8,128)S(1)}, u32[]{:S(2)}, u32[]{:S(2)}) collective-permute-start(f32[32,16]{1,0:T(8,128)S(1)} %get-tuple-element.21.refs_0_), channel_id=1, source_target_pairs={{1,0},{2,1},{3,2},{5,4},{6,5},{7,6},{9,8},{10,9},{11,10},{13,12},{... | collective-permute-start | bytes 6152 | tf_op jit(solution)/shard_map/ppermute | solution.py:403
  257.3 5.1 %collective-permute-start.6 = (f32[32,16]{1,0:T(8,128)S(1)}, f32[32,16]{1,0:T(8,128)S(1)}, u32[]{:S(2)}, u32[]{:S(2)}) collective-permute-start(f32[32,16]{1,0:T(8,128)S(1)} %get-tuple-element.21.refs_0_), channel_id=1, source_target_pairs={{0,1},{1,2},{2,3},{4,5},{5,6},{6,7},{8,9},{9,10},{10,11},{12,13},{... | collective-permute-start | bytes 6152 | tf_op jit(solution)/shard_map/ppermute | solution.py:402
  262.4 102.3 %copy-start.11 = (f32[1,1,32]{2,1,0:T(1,128)S(1)}, f32[1,1,32]{2,1,0:T(1,128)}, u32[]{:S(2)}) copy-start(f32[1,1,32]{2,1,0:T(1,128)} %param.15) | copy-start | bytes 388
  358.6 7.6 %collective-permute-start.9 = (f32[32,16]{1,0:T(8,128)S(1)}, f32[32,16]{1,0:T(8,128)S(1)}, u32[]{:S(2)}, u32[]{:S(2)}) collective-permute-start(f32[32,16]{1,0:T(8,128)S(1)} %get-tuple-element.24.refs_0_), channel_id=1, source_target_pairs={{1,0},{2,1},{3,2},{5,4},{6,5},{7,6},{9,8},{10,9},{11,10},{13,12},{... | collective-permute-start | bytes 6152 | tf_op jit(solution)/shard_map/ppermute | solution.py:403
  360.5 5.6 %collective-permute-start.8 = (f32[32,16]{1,0:T(8,128)S(1)}, f32[32,16]{1,0:T(8,128)S(1)}, u32[]{:S(2)}, u32[]{:S(2)}) collective-permute-start(f32[32,16]{1,0:T(8,128)S(1)} %get-tuple-element.24.refs_0_), channel_id=1, source_target_pairs={{0,1},{1,2},{2,3},{4,5},{5,6},{6,7},{8,9},{9,10},{10,11},{12,13},{... | collective-permute-start | bytes 6152 | tf_op jit(solution)/shard_map/ppermute | solution.py:402
  366.1 2.2 copy-start.3
  368.3 47.6 %copy-start.1 = (s32[2,32]{1,0:T(2,128)S(1)}, s32[2,32]{1,0:T(2,128)}, u32[]{:S(2)}) copy-start(s32[2,32]{1,0:T(2,128)} %param.12) | copy-start | bytes 772
  (1 other events, 2.0 us)

commit v2 on v1

--- a/solution.py
+++ b/solution.py
@@ -18,6 +18,7 @@
 EDGE = 2 * MARGIN
 LANES = 128
 GROUP = 8
+STACK = 8
 VMEM_LIMIT = 48 * 1024 * 1024
 
 f32 = jnp.float32
@@ -244,9 +245,14 @@
         foot_ref, side_ref = refs[:2]
         refs = refs[2:]
     if final:
-        (low_ref,) = refs
+        (low_ref,) = refs[:1]
+        refs = refs[1:]
     else:
-        new_foot_ref, new_side_ref, new_traces_ref, proj_ref, energy_ref = refs
+        new_foot_ref, new_side_ref, new_traces_ref = refs[:3]
+        refs = refs[3:]
+    back_ref, ahead_ref, back_side_ref, ahead_side_ref, scale_ref, side_scale_ref = refs[:6]
+    if not final:
+        proj_ref, energy_ref = refs[6:]
     size = GROUP * (cols + EDGE)
     side_size = (GROUP + 1) * LANES
     groups = obs_ref.shape[1] // size
@@ -254,106 +260,133 @@
     comps = traces_ref.shape[0]
     step = pl.program_id(0)
 
-    eye_at = lax.broadcasted_iota(jnp.int32, (volumes, volumes), 0)
-    eye = (eye_at == lax.broadcasted_iota(jnp.int32, (volumes, volumes), 1)).astype(f32).astype(bf16)
-
-    def prepared(ref):
-        full = ref[...]
-        low = full.astype(bf16)
-        flipped = nt_dot(eye, low).astype(bf16)
-        scale = 1.0 / (jnp.sum(full * full, axis=1, keepdims=True) + RIDGE)
-        return low, flipped, scale
-
-    own, own_t, own_scale = prepared(traces_ref)
-    left, left_t, left_scale = prepared(left_ref)
-    right, right_t, right_scale = prepared(right_ref)
-
-    if not final:
-
-        @pl.when(step == 0)
-        def _():
+    @pl.when(step == 0)
+    def _():
+        eye_at = lax.broadcasted_iota(jnp.int32, (volumes, volumes), 0)
+        eye_to = lax.broadcasted_iota(jnp.int32, (volumes, volumes), 1)
+        eye = (eye_at == eye_to).astype(f32).astype(bf16)
+
+        def spread(value):
+            rows, columns = value.shape
+            tiled = jnp.concatenate([value] * groups, axis=0)
+            tiled = jnp.concatenate([tiled] * groups, axis=1)
+            at = lax.broadcasted_iota(jnp.int32, tiled.shape, 0) // rows
+            to = lax.broadcasted_iota(jnp.int32, tiled.shape, 1) // columns
+            return jnp.where(at == to, tiled, 0.0).astype(bf16)
+
+        for which, ref in enumerate((traces_ref, left_ref, right_ref)):
+            full = ref[...]
+            low = full.astype(bf16)
+            flipped = nt_dot(eye, low)
+            ahead = spread(low.astype(f32))
+            back = spread(flipped)
+            scale = 1.0 / (jnp.sum(full * full, axis=1, keepdims=True) + RIDGE)
+            scale = jnp.concatenate([jnp.broadcast_to(scale, (comps, LANES))] * groups, axis=0)
+            if which == 0:
+                ahead_ref[...] = ahead
+                back_ref[...] = back
+                scale_ref[...] = scale
+            else:
+                part = (which - 1) * groups * comps
+                ahead_side_ref[part : part + groups * comps, :] = ahead
+                back_side_ref[:, part : part + groups * comps] = back
+                side_scale_ref[part : part + groups * comps, :] = scale
+        if not final:
             proj_ref[...] = jnp.zeros_like(proj_ref)
             energy_ref[...] = jnp.zeros_like(energy_ref)
 
-    def one_group(g, _):
-        at = pl.multiple_of(g * size, LANES)
-        side_at = pl.multiple_of(g * side_size, LANES)
-        base = lax.rem((step * groups + g) * GROUP, rows_patch).astype(f32)
-        if not final:
-            proj = proj_ref[...]
-            energy = energy_ref[...]
-        for j, (start, width) in enumerate(lane_pieces(cols)):
-            where = pl.ds(at + start, width)
-            side_where = pl.ds(side_at + j * LANES, LANES)
-            inside = pattern_ref[2:3, start : start + width]
-            is_left = pattern_ref[3:4, start : start + LANES]
-            is_right = pattern_ref[4:5, start : start + LANES]
-            obs = obs_ref[:, where].astype(f32)
-            if first:
+    back = back_ref[...]
+    ahead = ahead_ref[...]
+    back_side = back_side_ref[...]
+    ahead_side = ahead_side_ref[...]
+
+    def over_lanes(value, width):
+        return value if width == LANES else jnp.concatenate([value] * (width // LANES), axis=1)
+
+    def stacked(ref, starts, width):
+        return jnp.concatenate([ref[:, s : s + width] for s in starts], axis=0)
+
+    for j, (start, width) in enumerate(lane_pieces(cols)):
+        starts = [g * size + start for g in range(groups)]
+        side_starts = [g * side_size + j * LANES for g in range(groups)]
+        inside = pattern_ref[2:3, start : start + LANES]
+        is_left = pattern_ref[3:4, start : start + LANES]
+        is_right = pattern_ref[4:5, start : start + LANES]
+        obs = stacked(obs_ref, starts, width).astype(f32)
+        if first:
+            col = pattern_ref[1:2, start : start + width]
+            in_all = pattern_ref[2:3, start : start + width]
+            col_own = bump(col, centers_ref[:, 1:2]) * in_all
+            col = col[:, :LANES]
+            col_left = bump(col + cols, centers_ref[:, 3:4]) * is_left
+            col_right = bump(col - cols, centers_ref[:, 5:6]) * is_right
+            foot, side = [], []
+            for g in range(groups):
+                base = lax.rem((step * groups + g) * GROUP, rows_patch).astype(f32)
                 row = pattern_ref[0:1, start : start + width] + base
-                col = pattern_ref[1:2, start : start + width]
-                foot = bump(row, centers_ref[:, 0:1]) * (bump(col, centers_ref[:, 1:2]) * inside)
-                row, col = row[:, :LANES], col[:, :LANES]
-                side = bump(row, centers_ref[:, 2:3]) * (
-                    bump(col + cols, centers_ref[:, 3:4]) * is_left
-                ) + bump(row, centers_ref[:, 4:5]) * (
-                    bump(col - cols, centers_ref[:, 5:6]) * is_right
+                foot.append(bump(row, centers_ref[:, 0:1]) * col_own)
+                row = row[:, :LANES]
+                side.append(
+                    bump(row, centers_ref[:, 2:3]) * col_left
+                    + bump(row, centers_ref[:, 4:5]) * col_right
                 )
-            else:
-                foot = foot_ref[:, where]
-                side = side_ref[:, side_where]
-
-            def residual(foot_low, side):
-                model = jnp.dot(own_t, foot_low, preferred_element_type=f32)
-                extra = jnp.dot(left_t, (side * is_left).astype(bf16), preferred_element_type=f32)
-                extra = extra + jnp.dot(
-                    right_t, (side * is_right).astype(bf16), preferred_element_type=f32
-                )
-                head = model[:, :LANES] + extra
-                model = head if width == LANES else jnp.concatenate([head, model[:, LANES:]], axis=1)
-                return (obs - model).astype(bf16)
-
-            rest = residual(foot.astype(bf16), side)
-            update = jnp.dot(own, rest, preferred_element_type=f32)
-            foot = jnp.maximum(0.0, foot + inside * (update * own_scale))
-            foot_low = foot.astype(bf16)
-            if final:
-                low_ref[:, where] = foot_low
-                continue
-            update_left = jnp.dot(left, rest[:, :LANES], preferred_element_type=f32)
-            update_right = jnp.dot(right, rest[:, :LANES], preferred_element_type=f32)
-            side = jnp.maximum(
-                0.0,
-                side
-                + is_left * (update_left * left_scale)
-                + is_right * (update_right * right_scale),
-            )
-            new_foot_ref[:, where] = foot
-            new_side_ref[:, side_where] = side
-            proj = proj + nt_dot(foot_low, residual(foot_low, side))
-            square = foot * foot
-            for c in range(width // LANES):
-                energy = energy + square[:, c * LANES : (c + 1) * LANES]
-        if not final:
-            proj_ref[...] = proj
-            energy_ref[...] = energy
-        return 0
-
-    lax.fori_loop(0, groups, one_group, 0)
+            foot = jnp.concatenate(foot, axis=0)
+            side = jnp.concatenate(side, axis=0)
+        else:
+            foot = stacked(foot_ref, starts, width)
+            side = stacked(side_ref, side_starts, LANES)
+
+        def residual(foot_low, side):
+            model = jnp.dot(back, foot_low, preferred_element_type=f32)
+            sides = jnp.concatenate([side * is_left, side * is_right], axis=0).astype(bf16)
+            head = model[:, :LANES] + jnp.dot(back_side, sides, preferred_element_type=f32)
+            model = head if width == LANES else jnp.concatenate([head, model[:, LANES:]], axis=1)
+            return (obs - model).astype(bf16)
+
+        rest = residual(foot.astype(bf16), side)
+        update = jnp.dot(ahead, rest, preferred_element_type=f32) * over_lanes(scale_ref[...], width)
+        head = update[:, :LANES] * inside
+        update = head if width == LANES else jnp.concatenate([head, update[:, LANES:]], axis=1)
+        foot = jnp.maximum(0.0, foot + update)
+        foot_low = foot.astype(bf16)
+        if final:
+            for g, at in enumerate(starts):
+                low_ref[:, at : at + width] = foot_low[g * comps : (g + 1) * comps]
+            continue
+        sides = jnp.dot(ahead_side, rest[:, :LANES], preferred_element_type=f32)
+        sides = sides * side_scale_ref[...]
+        half = groups * comps
+        side = jnp.maximum(0.0, side + is_left * sides[:half] + is_right * sides[half:])
+        for g in range(groups):
+            part = slice(g * comps, (g + 1) * comps)
+            new_foot_ref[:, starts[g] : starts[g] + width] = foot[part]
+            new_side_ref[:, side_starts[g] : side_starts[g] + LANES] = side[part]
+        proj_ref[...] += nt_dot(foot_low, residual(foot_low, side))
+        square = foot * foot
+        energy = energy_ref[...]
+        for c in range(width // LANES):
+            energy = energy + square[:, c * LANES : (c + 1) * LANES]
+        energy_ref[...] = energy
 
     if not final:
 
         @pl.when(step == pl.num_programs(0) - 1)
         def _():
-            total = jnp.sum(energy_ref[...], axis=1, keepdims=True) + RIDGE
-            new_traces_ref[...] = jnp.maximum(0.0, traces_ref[...] + proj_ref[...] / total)
+            energy = jnp.sum(energy_ref[...], axis=1, keepdims=True)
+            total = RIDGE
+            proj = traces_ref[...] * 0.0
+            for g in range(groups):
+                part = slice(g * comps, (g + 1) * comps)
+                total = total + energy[part]
+                proj = proj + proj_ref[part, g * volumes : (g + 1) * volumes]
+            new_traces_ref[...] = jnp.maximum(0.0, traces_ref[...] + proj / total)
 
 
 def sweep(traces, left, right, pattern, centers, observed, state, rows_patch, cols, final):
     comps, volumes = traces.shape
     flat = observed.shape[1]
     groups_all = flat // (GROUP * (cols + EDGE))
-    per_block = 4
+    per_block = min(STACK, groups_all)
     blocks = groups_all // per_block
     size = per_block * GROUP * (cols + EDGE)
     side_size = per_block * (GROUP + 1) * LANES
@@ -384,7 +417,19 @@
             jax.ShapeDtypeStruct((comps, blocks * side_size), f32),
             jax.ShapeDtypeStruct((comps, volumes), f32),
         ]
-        scratch = [pltpu.VMEM((comps, volumes), f32), pltpu.VMEM((comps, LANES), f32)]
+        scratch = [
+            pltpu.VMEM((per_block * comps, per_block * volumes), f32),
+            pltpu.VMEM((per_block * comps, LANES), f32),
+        ]
+    tall, flat_tall = per_block * comps, per_block * volumes
+    scratch = [
+        pltpu.VMEM((flat_tall, tall), bf16),
+        pltpu.VMEM((tall, flat_tall), bf16),
+        pltpu.VMEM((flat_tall, 2 * tall), bf16),
+        pltpu.VMEM((2 * tall, flat_tall), bf16),
+        pltpu.VMEM((tall, LANES), f32),
+        pltpu.VMEM((2 * tall, LANES), f32),
+    ] + scratch
     return pl.pallas_call(
         functools.partial(sweep_kernel, rows_patch, cols, first, final),
         grid=(blocks,),

time: 417 us -> 245 us (0.59)
  Pallas kernels: 273 us -> 101 us
    pallas_call x3, Pallas kernels: 243 us -> 70.4 us  [sweep(): pl.pallas_call(functools.partial(sweep_kernel, rows_patch, cols, first, f...]
  transfers between devices with their start and end apart: 11 -> 11, of which waited for: 5 -> 5; matrix products, arithmetic and copies ran while one was open for 0% -> 1% of each run, Pallas kernels for 0% -> 0%
where the time goes in v2:
time: 245 us; the launch traced here: 244 us
  Pallas kernels  101 us (41%)
  waiting for transfers between devices  89.3 us (36%)
  starting transfers between devices  34.9 us (14%)
  blocking collectives  9.3 us (4%)
  local copies, waits for them, and re-layouts  8.34 us (3%)
    all_to_all x1, waiting for transfers between devices, shards(): lax.all_to_all(core, 'wide', split_axis=0, concat_axis=0, tiled=True)  83.8 us
    pallas_call x3, Pallas kernels, sweep(): pl.pallas_call(functools.partial(sweep_kernel, rows_patch, cols, first, f...  70.4 us
    pallas_call x1, Pallas kernels, observe(): pl.pallas_call(observe_kernel, grid=(PLANES, blocks), in_specs=[pl.BlockS...  17.1 us
    ppermute x4, starting transfers between devices, from_neighbours(): left = lax.ppermute(value, axis, [(i, i + 1) for i in range(count - 1)])  15.7 us
    ppermute x4, starting transfers between devices, from_neighbours(): right = lax.ppermute(value, axis, [(i + 1, i) for i in range(count - 1)])  11.8 us
    pallas_call x1, Pallas kernels, register(): pl.pallas_call(register_kernel, grid=(frames,), in_specs=[pl.BlockSpec(me...  9.52 us
    all_to_all x1, blocking collectives, shards(): lax.all_to_all(border, 'wide', split_axis=0, concat_axis=0, tiled=True)  9.3 us
    unnamed x30, local copies, waits for them, and re-layouts  7.86 us
  transfers between devices with their start and end apart: 11, of which 5 were waited for; matrix products, arithmetic and copies ran while one was open for 1% of the time, Pallas kernels for 0%

profile of v2, /device:TPU:1, one launch (start us, length us, event | category | flops | bytes accessed | tf_op | source)
XLA Modules:
  0.0 243.7 jit_solution(2672784863057856698)
XLA Ops:
  0.6 3.8 %pack_edges.1 = (bf16[512,128]{1,0:T(8,128)(2,1)}, bf16[512,128]{1,0:T(8,128)(2,1)}) custom-call(bf16[8,512,512]{2,1,0:T(8,128)(2,1)} %frame_ref.1, bf16[8,512,512]{2,1,0:T(8,128)(2,1)} %frame_ref.1), custom_call_target="tpu_custom_call" | custom-call | tf_op jit(solution)/shard_map/pack_edges/pallas_call | solution.py:54
  4.5 2.6 %collective-permute-start.1 = (bf16[512,128]{1,0:T(8,128)(2,1)}, bf16[512,128]{1,0:T(8,128)(2,1)S(1)}, u32[]{:S(2)}, u32[]{:S(2)}) collective-permute-start(bf16[512,128]{1,0:T(8,128)(2,1)} %get-tuple-element.16), channel_id=1, source_target_pairs={{0,1},{1,2},{2,3},{3,0},{4,5},{5,6},{6,7},{7,4},{8,9},{9,10},{10,1... | collective-permute-start | bytes 393224 | tf_op jit(solution)/shard_map/ppermute | solution.py:462
  7.2 3.6 %collective-permute-done.head_ref = bf16[512,128]{1,0:T(8,128)(2,1)S(1)} collective-permute-done((bf16[512,128]{1,0:T(8,128)(2,1)}, bf16[512,128]{1,0:T(8,128)(2,1)S(1)}, u32[]{:S(2)}, u32[]{:S(2)}) %collective-permute-start) | collective-permute-done | bytes 131104 | tf_op jit(solution)/shard_map/ppermute | solution.py:463
  10.7 9.5 %register.1 = (bf16[4,8,128,512]{3,2,1,0:T(8,128)(2,1)S(1)}, bf16[4,128,128]{2,1,0:T(8,128)(2,1)S(1)}) custom-call(s32[2,8]{1,0:T(2,128)S(1)} %constant_dynamic-slice_fusion.shifts_ref, bf16[8,512,512]{2,1,0:T(8,128)(2,1)} %frame_ref.1, bf16[512,128]{1,0:T(8,128)(2,1)S(1)} %collective-permute-done.head_ref, bf16[512,128]{1,0:T(8,128)(2,1)S(1)} %collective-permute-done.1.tail_ref), custom_call_target="tpu_custom_call" | custom-call | tf_op jit(solution)/shard_map/register/pallas_call | solution.py:101
  20.3 2.0 copy-done.4
  22.3 9.3 %all_to_all.10.border_ref = bf16[4,128,128]{2,1,0:T(8,128)(2,1)S(1)} all-to-all(bf16[4,128,128]{2,1,0:T(8,128)(2,1)S(1)} %get-tuple-element.18), channel_id=1, replica_groups=mesh['parts'=2,'wide'=4,'narrow'=4] {'wide'}, dimensions={0} | all-to-all | bytes 262144 | tf_op jit(solution)/shard_map/all_to_all | solution.py:467
  31.6 4.9 %all-to-all-start = ((bf16[4,8,128,512]{3,2,1,0:T(8,128)(2,1)}), bf16[4,8,128,512]{3,2,1,0:T(8,128)(2,1)}, u32[]{:S(2)}, u32[]{:S(2)}) async-start(bf16[4,8,128,512]{3,2,1,0:T(8,128)(2,1)} %copy-done.4), calls=%async_computation | async-start | bytes 8388608 | tf_op jit(solution)/shard_map/all_to_all | solution.py:466
  36.6 4.6 %collective-permute-start.3 = (f32[32,2]{1,0:T(8,128)S(1)}, f32[32,2]{1,0:T(8,128)S(1)}, u32[]{:S(2)}, u32[]{:S(2)}) collective-permute-start(f32[32,2]{1,0:T(8,128)S(1)} %convert_element_type.4), channel_id=1, source_target_pairs={{1,0},{2,1},{3,2},{5,4},{6,5},{7,6},{9,8},{10,9},{11,10},{13,12},{... | collective-permute-start | bytes 776 | tf_op jit(solution)/shard_map/ppermute | solution.py:448
  41.2 3.2 %collective-permute-start.2 = (f32[32,2]{1,0:T(8,128)S(1)}, f32[32,2]{1,0:T(8,128)S(1)}, u32[]{:S(2)}, u32[]{:S(2)}) collective-permute-start(f32[32,2]{1,0:T(8,128)S(1)} %convert_element_type.4), channel_id=1, source_target_pairs={{0,1},{1,2},{2,3},{4,5},{5,6},{6,7},{8,9},{9,10},{10,11},{12,13},{... | collective-permute-start | bytes 776 | tf_op jit(solution)/shard_map/ppermute | solution.py:447
  45.4 83.8 %all-to-all-done = bf16[4,8,128,512]{3,2,1,0:T(8,128)(2,1)} async-done(((bf16[4,8,128,512]{3,2,1,0:T(8,128)(2,1)}), bf16[4,8,128,512]{3,2,1,0:T(8,128)(2,1)}, u32[]{:S(2)}, u32[]{:S(2)}) %all-to-all-start) | async-done | bytes 4194336 | tf_op jit(solution)/shard_map/all_to_all | solution.py:466
  129.2 17.1 %observe.1 = (bf16[16,135168]{1,0:T(8,128)(2,1)}, f32[32,16]{1,0:T(8,128)S(1)}) custom-call(bf16[256,256]{1,0:T(8,128)(2,1)S(1)} %copy-done.5, bf16[32,128,512]{2,1,0:T(8,128)(2,1)} %bitcast.recv_ref, bf16[4,128,128]{2,1,0:T(8,128)(2,1)S(1)} %all_to_all.10.border_ref, f32[8,4224]{1,0:T(8,128)S(1)} %stack.34.pattern_ref.refs_3_, ...), custom_call_target="tpu_custom_call" | custom-call | tf_op jit(solution)/shard_map/observe/pallas_call | solution.py:217
  146.3 3.4 %collective-permute-start.5 = (f32[32,16]{1,0:T(8,128)S(1)}, f32[32,16]{1,0:T(8,128)S(1)}, u32[]{:S(2)}, u32[]{:S(2)}) collective-permute-start(f32[32,16]{1,0:T(8,128)S(1)} %get-tuple-element.19.refs_0_), channel_id=1, source_target_pairs={{1,0},{2,1},{3,2},{5,4},{6,5},{7,6},{9,8},{10,9},{11,10},{13,12},{... | collective-permute-start | bytes 6152 | tf_op jit(solution)/shard_map/ppermute | solution.py:448
  149.7 3.8 %collective-permute-start.4 = (f32[32,16]{1,0:T(8,128)S(1)}, f32[32,16]{1,0:T(8,128)S(1)}, u32[]{:S(2)}, u32[]{:S(2)}) collective-permute-start(f32[32,16]{1,0:T(8,128)S(1)} %get-tuple-element.19.refs_0_), channel_id=1, source_target_pairs={{0,1},{1,2},{2,3},{4,5},{5,6},{6,7},{8,9},{9,10},{10,11},{12,13},{... | collective-permute-start | bytes 6152 | tf_op jit(solution)/shard_map/ppermute | solution.py:447
  153.5 0.8 collective-permute-done.4.refs_1_
  154.4 2.2 copy-done.2
  156.6 27.9 %sweep.3 = (f32[32,135168]{1,0:T(8,128)}, f32[32,36864]{1,0:T(8,128)}, f32[32,16]{1,0:T(8,128)S(1)}) custom-call(f32[32,16]{1,0:T(8,128)S(1)} %get-tuple-element.19.refs_0_, f32[32,16]{1,0:T(8,128)S(1)} %collective-permute-done.4.refs_1_, f32[32,16]{1,0:T(8,128)S(1)} %collective-permute-done.5.refs_2_, f32[8,4224]{1,0:T(8,128)S(1)} %stack.34.pattern_ref.refs_3_, ...), custom_call_target="tpu_custom_call" | custom-call | tf_op jit(solution)/shard_map/sweep/pallas_call | solution.py:433
  184.5 1.9 collective-permute-start.7
  186.4 4.4 %collective-permute-start.6 = (f32[32,16]{1,0:T(8,128)S(1)}, f32[32,16]{1,0:T(8,128)S(1)}, u32[]{:S(2)}, u32[]{:S(2)}) collective-permute-start(f32[32,16]{1,0:T(8,128)S(1)} %get-tuple-element.21.refs_0_), channel_id=1, source_target_pairs={{0,1},{1,2},{2,3},{4,5},{5,6},{6,7},{8,9},{9,10},{10,11},{12,13},{... | collective-permute-start | bytes 6152 | tf_op jit(solution)/shard_map/ppermute | solution.py:447
  191.4 27.0 %sweep.4 = (f32[32,135168]{1,0:T(8,128)}, f32[32,36864]{1,0:T(8,128)}, f32[32,16]{1,0:T(8,128)S(1)}) custom-call(f32[32,16]{1,0:T(8,128)S(1)} %get-tuple-element.21.refs_0_, f32[32,16]{1,0:T(8,128)S(1)} %collective-permute-done.6.refs_1_, f32[32,16]{1,0:T(8,128)S(1)} %collective-permute-done.7.refs_2_, f32[8,4224]{1,0:T(8,128)S(1)} %stack.34.pattern_ref.refs_3_, ...), custom_call_target="tpu_custom_call" | custom-call | tf_op jit(solution)/shard_map/sweep/pallas_call | solution.py:433
  218.4 1.9 collective-permute-start.9
  220.4 4.2 %collective-permute-start.8 = (f32[32,16]{1,0:T(8,128)S(1)}, f32[32,16]{1,0:T(8,128)S(1)}, u32[]{:S(2)}, u32[]{:S(2)}) collective-permute-start(f32[32,16]{1,0:T(8,128)S(1)} %get-tuple-element.24.refs_0_), channel_id=1, source_target_pairs={{0,1},{1,2},{2,3},{4,5},{5,6},{6,7},{8,9},{9,10},{10,11},{12,13},{... | collective-permute-start | bytes 6152 | tf_op jit(solution)/shard_map/ppermute | solution.py:447
  224.7 0.7 copy.19
  226.0 2.2 copy-done.3
  228.2 15.5 %sweep.5 = bf16[32,135168]{1,0:T(8,128)(2,1)} custom-call(f32[32,16]{1,0:T(8,128)S(1)} %get-tuple-element.24.refs_0_, f32[32,16]{1,0:T(8,128)S(1)} %collective-permute-done.8.refs_1_, f32[32,16]{1,0:T(8,128)S(1)} %collective-permute-done.9.refs_2_, f32[8,4224]{1,0:T(8,128)S(1)} %stack.34.pattern_ref.refs_3_, ...), custom_call_target="tpu_custom_call" | custom-call | tf_op jit(solution)/shard_map/sweep/pallas_call | solution.py:433
  (51 shorter events, 2.5 us)
Async XLA Ops:
  0.6 6.5 %copy-start = (s32[2,32]{1,0:T(2,128)S(1)}, s32[2,32]{1,0:T(2,128)}, u32[]{:S(2)}) copy-start(s32[2,32]{1,0:T(2,128)} %param.12) | copy-start | bytes 772
  4.4 6.3 %collective-permute-start = (bf16[512,128]{1,0:T(8,128)(2,1)}, bf16[512,128]{1,0:T(8,128)(2,1)S(1)}, u32[]{:S(2)}, u32[]{:S(2)}) collective-permute-start(bf16[512,128]{1,0:T(8,128)(2,1)} %get-tuple-element.15), channel_id=1, source_target_pairs={{1,0},{2,1},{3,2},{0,3},{5,4},{6,5},{7,6},{4,7},{9,8},{10,9},{11,1... | collective-permute-start | bytes 393224 | tf_op jit(solution)/shard_map/ppermute | solution.py:463
  4.5 6.2 %collective-permute-start.1 = (bf16[512,128]{1,0:T(8,128)(2,1)}, bf16[512,128]{1,0:T(8,128)(2,1)S(1)}, u32[]{:S(2)}, u32[]{:S(2)}) collective-permute-start(bf16[512,128]{1,0:T(8,128)(2,1)} %get-tuple-element.16), channel_id=1, source_target_pairs={{0,1},{1,2},{2,3},{3,0},{4,5},{5,6},{6,7},{7,4},{8,9},{9,10},{10,1... | collective-permute-start | bytes 393224 | tf_op jit(solution)/shard_map/ppermute | solution.py:462
  22.3 14.2 %copy-start.12 = (s32[1,1,32]{2,1,0:T(1,128)S(1)}, s32[1,1,32]{2,1,0:T(1,128)}, u32[]{:S(2)}) copy-start(s32[1,1,32]{2,1,0:T(1,128)} %param.14) | copy-start | bytes 388
  22.3 14.2 %copy-start.13 = (s32[1,1,32]{2,1,0:T(1,128)S(1)}, s32[1,1,32]{2,1,0:T(1,128)}, u32[]{:S(2)}) copy-start(s32[1,1,32]{2,1,0:T(1,128)} %param.13) | copy-start | bytes 388
  22.3 22.2 %copy-start.6 = (s32[4224]{0:T(1024)S(1)}, s32[4224]{0:T(1024)}, u32[]{:S(2)}) copy-start(s32[4224]{0:T(1024)} %constant.38.clone) | copy-start | bytes 50692
  22.3 22.2 %copy-start.7 = (f32[4224]{0:T(1024)S(1)}, f32[4224]{0:T(1024)}, u32[]{:S(2)}) copy-start(f32[4224]{0:T(1024)} %constant.40.clone) | copy-start | bytes 50692
  22.3 22.2 %copy-start.8 = (f32[4224]{0:T(1024)S(1)}, f32[4224]{0:T(1024)}, u32[]{:S(2)}) copy-start(f32[4224]{0:T(1024)} %constant.39.clone) | copy-start | bytes 50692
  22.3 22.4 %copy-start.9 = (f32[1,4224]{1,0:T(1,128)S(1)}, f32[1,4224]{1,0:T(1,128)}, u32[]{:S(2)}) copy-start(f32[1,4224]{1,0:T(1,128)} %constant.50) | copy-start | bytes 50692
  22.3 22.4 %copy-start.10 = (f32[1,4224]{1,0:T(1,128)S(1)}, f32[1,4224]{1,0:T(1,128)}, u32[]{:S(2)}) copy-start(f32[1,4224]{1,0:T(1,128)} %constant.49) | copy-start | bytes 50692
  22.3 106.9 %copy-start.5 = (bf16[256,256]{1,0:T(8,128)(2,1)S(1)}, bf16[256,256]{1,0:T(8,128)(2,1)}, u32[]{:S(2)}) copy-start(bf16[256,256]{1,0:T(8,128)(2,1)} %constant.43.clone.mix_ref) | copy-start | bytes 393220
  31.6 97.5 %all-to-all-start = ((bf16[4,8,128,512]{3,2,1,0:T(8,128)(2,1)}), bf16[4,8,128,512]{3,2,1,0:T(8,128)(2,1)}, u32[]{:S(2)}, u32[]{:S(2)}) async-start(bf16[4,8,128,512]{3,2,1,0:T(8,128)(2,1)} %copy-done.4), calls=%async_computation | async-start | bytes 8388608 | tf_op jit(solution)/shard_map/all_to_all | solution.py:466
  36.6 8.3 %collective-permute-start.3 = (f32[32,2]{1,0:T(8,128)S(1)}, f32[32,2]{1,0:T(8,128)S(1)}, u32[]{:S(2)}, u32[]{:S(2)}) collective-permute-start(f32[32,2]{1,0:T(8,128)S(1)} %convert_element_type.4), channel_id=1, source_target_pairs={{1,0},{2,1},{3,2},{5,4},{6,5},{7,6},{9,8},{10,9},{11,10},{13,12},{... | collective-permute-start | bytes 776 | tf_op jit(solution)/shard_map/ppermute | solution.py:448
  41.2 4.1 %collective-permute-start.2 = (f32[32,2]{1,0:T(8,128)S(1)}, f32[32,2]{1,0:T(8,128)S(1)}, u32[]{:S(2)}, u32[]{:S(2)}) collective-permute-start(f32[32,2]{1,0:T(8,128)S(1)} %convert_element_type.4), channel_id=1, source_target_pairs={{0,1},{1,2},{2,3},{4,5},{5,6},{6,7},{8,9},{9,10},{10,11},{12,13},{... | collective-permute-start | bytes 776 | tf_op jit(solution)/shard_map/ppermute | solution.py:447
  146.3 7.2 %collective-permute-start.5 = (f32[32,16]{1,0:T(8,128)S(1)}, f32[32,16]{1,0:T(8,128)S(1)}, u32[]{:S(2)}, u32[]{:S(2)}) collective-permute-start(f32[32,16]{1,0:T(8,128)S(1)} %get-tuple-element.19.refs_0_), channel_id=1, source_target_pairs={{1,0},{2,1},{3,2},{5,4},{6,5},{7,6},{9,8},{10,9},{11,10},{13,12},{... | collective-permute-start | bytes 6152 | tf_op jit(solution)/shard_map/ppermute | solution.py:448
  149.7 4.7 %collective-permute-start.4 = (f32[32,16]{1,0:T(8,128)S(1)}, f32[32,16]{1,0:T(8,128)S(1)}, u32[]{:S(2)}, u32[]{:S(2)}) collective-permute-start(f32[32,16]{1,0:T(8,128)S(1)} %get-tuple-element.19.refs_0_), channel_id=1, source_target_pairs={{0,1},{1,2},{2,3},{4,5},{5,6},{6,7},{8,9},{9,10},{10,11},{12,13},{... | collective-permute-start | bytes 6152 | tf_op jit(solution)/shard_map/ppermute | solution.py:447
  154.4 2.2 copy-start.2
  184.5 6.3 %collective-permute-start.7 = (f32[32,16]{1,0:T(8,128)S(1)}, f32[32,16]{1,0:T(8,128)S(1)}, u32[]{:S(2)}, u32[]{:S(2)}) collective-permute-start(f32[32,16]{1,0:T(8,128)S(1)} %get-tuple-element.21.refs_0_), channel_id=1, source_target_pairs={{1,0},{2,1},{3,2},{5,4},{6,5},{7,6},{9,8},{10,9},{11,10},{13,12},{... | collective-permute-start | bytes 6152 | tf_op jit(solution)/shard_map/ppermute | solution.py:448
  186.4 5.1 %collective-permute-start.6 = (f32[32,16]{1,0:T(8,128)S(1)}, f32[32,16]{1,0:T(8,128)S(1)}, u32[]{:S(2)}, u32[]{:S(2)}) collective-permute-start(f32[32,16]{1,0:T(8,128)S(1)} %get-tuple-element.21.refs_0_), channel_id=1, source_target_pairs={{0,1},{1,2},{2,3},{4,5},{5,6},{6,7},{8,9},{9,10},{10,11},{12,13},{... | collective-permute-start | bytes 6152 | tf_op jit(solution)/shard_map/ppermute | solution.py:447
  191.4 33.1 %copy-start.11 = (f32[1,1,32]{2,1,0:T(1,128)S(1)}, f32[1,1,32]{2,1,0:T(1,128)}, u32[]{:S(2)}) copy-start(f32[1,1,32]{2,1,0:T(1,128)} %param.15) | copy-start | bytes 388
  218.4 7.6 %collective-permute-start.9 = (f32[32,16]{1,0:T(8,128)S(1)}, f32[32,16]{1,0:T(8,128)S(1)}, u32[]{:S(2)}, u32[]{:S(2)}) collective-permute-start(f32[32,16]{1,0:T(8,128)S(1)} %get-tuple-element.24.refs_0_), channel_id=1, source_target_pairs={{1,0},{2,1},{3,2},{5,4},{6,5},{7,6},{9,8},{10,9},{11,10},{13,12},{... | collective-permute-start | bytes 6152 | tf_op jit(solution)/shard_map/ppermute | solution.py:448
  220.4 5.7 %collective-permute-start.8 = (f32[32,16]{1,0:T(8,128)S(1)}, f32[32,16]{1,0:T(8,128)S(1)}, u32[]{:S(2)}, u32[]{:S(2)}) collective-permute-start(f32[32,16]{1,0:T(8,128)S(1)} %get-tuple-element.24.refs_0_), channel_id=1, source_target_pairs={{0,1},{1,2},{2,3},{4,5},{5,6},{6,7},{8,9},{9,10},{10,11},{12,13},{... | collective-permute-start | bytes 6152 | tf_op jit(solution)/shard_map/ppermute | solution.py:447
  226.0 2.2 copy-start.3
  228.2 15.5 %copy-start.1 = (s32[2,32]{1,0:T(2,128)S(1)}, s32[2,32]{1,0:T(2,128)}, u32[]{:S(2)}) copy-start(s32[2,32]{1,0:T(2,128)} %param.12) | copy-start | bytes 772
  (1 other events, 2.0 us)

commit v3 on v2

--- a/solution.py
+++ b/solution.py
@@ -18,7 +18,9 @@
 EDGE = 2 * MARGIN
 LANES = 128
 GROUP = 8
+ROWS = 16
 STACK = 8
+CHUNKS = 2
 VMEM_LIMIT = 48 * 1024 * 1024
 
 f32 = jnp.float32
@@ -64,10 +66,23 @@
     )(recording, recording)
 
 
-def register_kernel(shifts_ref, frame_ref, head_ref, tail_ref, core_ref, border_ref, acc_ref):
+def extra_rows(rows_chunk, cols):
+    return -(-(rows_chunk // ROWS) // (cols // LANES)) * ROWS
+
+
+def frames_of(ref, rows_chunk, cols):
+    return (ref.shape[1] - extra_rows(rows_chunk, cols)) // rows_chunk
+
+
+def register_kernel(shifts_ref, frame_ref, head_ref, tail_ref, *refs):
+    out_refs, acc_ref = refs[:-1], refs[-1]
     f = pl.program_id(0)
-    wide, _, rows_patch, cols = core_ref.shape
-    height = wide * rows_patch
+    frames = pl.num_programs(0)
+    _, height, cols = frame_ref.shape
+    wide = out_refs[0].shape[0]
+    rows_patch = height // wide
+    rows_chunk = rows_patch // len(out_refs)
+    across = cols // LANES
     width = cols + LANES
     lane = lane_iota((height, LANES))
     back = lax.rem(LANES - f * EDGE, LANES)
@@ -79,7 +94,10 @@
     col_move = lax.rem(shifts_ref[1, f] + width, width)
     frame = pltpu.roll(frame, row_move, 0)
     frame = pltpu.roll(frame, col_move, 1)
-    core_ref[...] = frame[:, :cols].astype(bf16).reshape(wide, 1, rows_patch, cols)
+    core = frame[:, :cols].astype(bf16).reshape(wide, rows_patch, cols)
+    for c, ref in enumerate(out_refs):
+        at = pl.ds(pl.multiple_of(f * rows_chunk, ROWS), rows_chunk)
+        ref[:, at, :] = core[:, c * rows_chunk : (c + 1) * rows_chunk]
     moved = pltpu.roll(frame[:, cols:], lax.rem(f * EDGE + MARGIN, LANES), 1)
     here = (lane >= f * EDGE) & (lane < (f + 1) * EDGE)
 
@@ -89,14 +107,21 @@
 
     acc_ref[...] = jnp.where(here, moved, acc_ref[...])
 
-    @pl.when(f == pl.num_programs(0) - 1)
+    @pl.when(f == frames - 1)
     def _():
-        border_ref[...] = acc_ref[...].astype(bf16).reshape(border_ref.shape)
-
-
-def register(shifts, recording, head, tail, wide):
+        border = acc_ref[...].astype(bf16).reshape(wide, rows_patch, LANES)
+        for c, ref in enumerate(out_refs):
+            for k in range(rows_chunk // ROWS):
+                at = c * rows_chunk + k * ROWS
+                row = frames_of(ref, rows_chunk, cols) * rows_chunk + k // across * ROWS
+                lane_at = k % across * LANES
+                ref[:, row : row + ROWS, lane_at : lane_at + LANES] = border[:, at : at + ROWS]
+
+
+def register(shifts, recording, head, tail, wide, chunks):
     frames, height, cols = recording.shape
-    rows_patch = height // wide
+    rows_chunk = height // wide // chunks
+    shape = (wide, frames * rows_chunk + extra_rows(rows_chunk, cols), cols)
     whole = pl.BlockSpec((height, LANES), lambda f: (0, 0))
     return pl.pallas_call(
         register_kernel,
@@ -107,14 +132,8 @@
             whole,
             whole,
         ],
-        out_specs=[
-            pl.BlockSpec((wide, 1, rows_patch, cols), lambda f: (0, f, 0, 0)),
-            pl.BlockSpec((wide, rows_patch, LANES), lambda f: (0, 0, 0)),
-        ],
-        out_shape=[
-            jax.ShapeDtypeStruct((wide, frames, rows_patch, cols), bf16),
-            jax.ShapeDtypeStruct((wide, rows_patch, LANES), bf16),
-        ],
+        out_specs=[pl.BlockSpec(shape, lambda f: (0, 0, 0))] * chunks,
+        out_shape=[jax.ShapeDtypeStruct(shape, bf16)] * chunks,
         scratch_shapes=[pltpu.VMEM((height, LANES), f32)],
         compiler_params=pltpu.CompilerParams(vmem_limit_bytes=VMEM_LIMIT),
         name="register",
@@ -137,23 +156,34 @@
 
 
 def observe_kernel(
-    mix_ref, recv_ref, border_ref, pattern_ref, centers_ref, obs_ref, traces_ref, proj_ref, energy_ref
+    chunk, rows_chunk, mix_ref, recv_ref, pattern_ref, centers_ref, proj_in, energy_in, *refs
 ):
-    volumes, rows, cols = recv_ref.shape
-    sources = border_ref.shape[0]
+    obs_ref, traces_ref, proj_ref, energy_ref = refs[-4:]
+    volumes, rows = VOLUMES, ROWS
+    sources, _, cols = recv_ref.shape
     per_source = volumes // sources
-    step = pl.program_id(0) * pl.num_programs(1) + pl.program_id(1)
+    across = cols // LANES
+    y = pl.program_id(1)
+    step = pl.program_id(0) * pl.num_programs(1) + y
     last = pl.num_programs(0) * pl.num_programs(1) - 1
-    base = (pl.program_id(1) * rows).astype(f32)
+    base = (chunk * rows_chunk + y * rows).astype(f32)
     mix = mix_ref[...]
 
     @pl.when(step == 0)
     def _():
-        proj_ref[...] = jnp.zeros_like(proj_ref)
-        energy_ref[...] = jnp.zeros_like(energy_ref)
-
-    core = jnp.dot(mix, recv_ref[...].reshape(volumes * rows, cols), preferred_element_type=f32)
-    strips = [border_ref[s].astype(f32) for s in range(sources)]
+        proj_ref[...] = proj_in[...]
+        energy_ref[...] = energy_in[...]
+
+    def frame_rows(v):
+        row = (v % per_source) * rows_chunk + y * rows
+        return recv_ref[v // per_source, pl.ds(pl.multiple_of(row, rows), rows), :]
+
+    border_at = per_source * rows_chunk + y // across * rows
+    border_at = pl.ds(pl.multiple_of(border_at, rows), rows)
+    lanes_at = pl.ds(pl.multiple_of(lax.rem(y, across) * LANES, LANES), LANES)
+    received = jnp.concatenate([frame_rows(v) for v in range(volumes)], axis=0)
+    core = jnp.dot(mix, received, preferred_element_type=f32)
+    strips = [recv_ref[s, border_at, lanes_at].astype(f32) for s in range(sources)]
     border = jnp.concatenate(
         [
             roll_lanes(strips[v // per_source], -(v % per_source) * EDGE - MARGIN)
@@ -203,39 +233,55 @@
         traces_ref[...] = jnp.maximum(0.0, proj / total)
 
 
-def observe(received, border, pattern, centers, frames):
-    _, rows_patch, cols = received.shape
+def observe(received, pattern, centers, earlier, rows_patch, chunk, chunks):
+    devices, rows_all, cols = received.shape
     comps = centers.shape[0]
-    rows = 16
-    blocks = rows_patch // rows
-    sources = border.shape[0] // PLANES
+    rows_chunk = rows_patch // chunks
+    blocks = rows_chunk // ROWS
+    sources = devices // PLANES
     size = GROUP * (cols + EDGE)
-    same = np.eye(rows)
-    mix = np.einsum("yx,vu->yvux", same, np.eye(VOLUMES) - 1.0 / VOLUMES)
-    mix = jnp.asarray(mix.reshape(rows * VOLUMES, VOLUMES * rows), bf16)
+    mix = np.einsum("yx,vu->yvux", np.eye(ROWS), np.eye(VOLUMES) - 1.0 / VOLUMES)
+    mix = jnp.asarray(mix.reshape(ROWS * VOLUMES, VOLUMES * ROWS), bf16)
     flat = PLANES * rows_patch * (cols + EDGE)
+    small = pl.BlockSpec((comps, VOLUMES), lambda p, y: (0, 0))
+    wide_small = pl.BlockSpec((comps, LANES), lambda p, y: (0, 0))
+    if earlier is None:
+        rest = [jnp.zeros((comps, VOLUMES), f32), jnp.zeros((comps, LANES), f32)]
+        aliases = {}
+    else:
+        rest = [earlier[2], earlier[3], earlier[0]]
+        aliases = {6: 0}
     return pl.pallas_call(
-        observe_kernel,
+        functools.partial(observe_kernel, chunk, rows_chunk),
         grid=(PLANES, blocks),
         in_specs=[
             pl.BlockSpec(mix.shape, lambda p, y: (0, 0)),
-            pl.BlockSpec((VOLUMES, rows, cols), lambda p, y: (p, y, 0)),
-            pl.BlockSpec((sources, rows, LANES), lambda p, y: (p, y, 0)),
+            pl.BlockSpec((sources, rows_all, cols), lambda p, y: (p, 0, 0)),
             pl.BlockSpec((8, size), lambda p, y: (0, 0)),
-            pl.BlockSpec((comps, LANES), lambda p, y: (0, 0)),
-        ],
+            wide_small,
+            small,
+            wide_small,
+        ]
+        + [pl.BlockSpec(memory_space=pl.ANY)] * len(aliases),
         out_specs=[
-            pl.BlockSpec((VOLUMES, rows * (cols + EDGE)), lambda p, y: (0, p * blocks + y)),
-            pl.BlockSpec((comps, VOLUMES), lambda p, y: (0, 0)),
+            pl.BlockSpec(
+                (VOLUMES, ROWS * (cols + EDGE)),
+                lambda p, y: (0, (p * chunks + chunk) * blocks + y),
+            ),
+            small,
+            small,
+            wide_small,
         ],
         out_shape=[
             jax.ShapeDtypeStruct((VOLUMES, flat), bf16),
             jax.ShapeDtypeStruct((comps, VOLUMES), f32),
+            jax.ShapeDtypeStruct((comps, VOLUMES), f32),
+            jax.ShapeDtypeStruct((comps, LANES), f32),
         ],
-        scratch_shapes=[pltpu.VMEM((comps, VOLUMES), f32), pltpu.VMEM((comps, LANES), f32)],
+        input_output_aliases=aliases,
         compiler_params=pltpu.CompilerParams(vmem_limit_bytes=VMEM_LIMIT),
         name="observe",
-    )(mix, received, border, pattern, centers)
+    )(mix, received, pattern, centers, *rest)
 
 
 def sweep_kernel(rows_patch, cols, first, final, *refs):
@@ -462,10 +508,11 @@
     tail = lax.ppermute(tail, "narrow", ring)
     head = lax.ppermute(head, "narrow", [(b, a) for a, b in ring])
     shifts = lax.dynamic_slice_in_dim(offsets, lax.axis_index("wide") * frames_dev, frames_dev, 1)
-    core, border = register(shifts, recording, head, tail, wide)
-    received = lax.all_to_all(core, "wide", split_axis=0, concat_axis=0, tiled=True)
-    border = lax.all_to_all(border, "wide", split_axis=0, concat_axis=0, tiled=True)
-    received = received.reshape(wide * frames_dev, rows_patch, cols)
+    chunks = CHUNKS if rows_patch % (CHUNKS * ROWS) == 0 else 1
+    received = [
+        lax.all_to_all(part, "wide", split_axis=0, concat_axis=0, tiled=True)
+        for part in register(shifts, recording, head, tail, wide, chunks)
+    ]
 
     place = np.arange(GROUP * ext_width)
     row = place // ext_width
@@ -484,7 +531,10 @@
         [centers, left, right, jnp.zeros((comps, LANES - 6), f32)], axis=1
     )
 
-    observed, traces = observe(received, border, pattern, centers, frames_dev)
+    earlier = None
+    for chunk in range(chunks):
+        earlier = observe(received[chunk], pattern, centers, earlier, rows_patch, chunk, chunks)
+    observed, traces = earlier[:2]
     state = None
     for turn in range(ITERS):
         left, right = from_neighbours(traces, "narrow")

time: 245 us -> 233 us (0.951)
  waiting for transfers between devices: 89.3 us -> 36.5 us
  blocking collectives: 9.3 us -> 53.5 us
    all_to_all x1, waiting for transfers between devices: 83.8 us -> 31.1 us  [shards(): lax.all_to_all(part, 'wide', split_axis=0, concat_axis=0, tiled=True)]
    all_to_all x1, blocking collectives: 9.3 us -> 53.5 us  [shards(): lax.all_to_all(part, 'wide', split_axis=0, concat_axis=0, tiled=True)]
    pallas_call x1 -> x2, Pallas kernels: 17.1 us -> 15.8 us  [observe(): pl.pallas_call(functools.partial(observe_kernel, chunk, rows_chunk), grid...]
    unnamed x30 -> x32, local copies, waits for them, and re-layouts: 7.86 us -> 7.47 us
  transfers between devices with their start and end apart: 11 -> 11, of which waited for: 5 -> 5; matrix products, arithmetic and copies ran while one was open for 1% -> 1% of each run, Pallas kernels for 0% -> 3%
where the time goes in v3:
time: 233 us; the launch traced here: 232 us
  Pallas kernels  99.2 us (43%)
  blocking collectives  53.5 us (23%)
  waiting for transfers between devices  36.5 us (16%)
  starting transfers between devices  33.4 us (14%)
  local copies, waits for them, and re-layouts  7.96 us (3%)
    pallas_call x3, Pallas kernels, sweep(): pl.pallas_call(functools.partial(sweep_kernel, rows_patch, cols, first, f...  70.4 us
    all_to_all x1, blocking collectives, shards(): lax.all_to_all(part, 'wide', split_axis=0, concat_axis=0, tiled=True)  53.5 us
    all_to_all x1, waiting for transfers between devices, shards(): lax.all_to_all(part, 'wide', split_axis=0, concat_axis=0, tiled=True)  31.1 us
    ppermute x4, starting transfers between devices, from_neighbours(): left = lax.ppermute(value, axis, [(i, i + 1) for i in range(count - 1)])  16.3 us
    pallas_call x2, Pallas kernels, observe(): pl.pallas_call(functools.partial(observe_kernel, chunk, rows_chunk), grid...  15.8 us
    ppermute x4, starting transfers between devices, from_neighbours(): right = lax.ppermute(value, axis, [(i + 1, i) for i in range(count - 1)])  10.8 us
    pallas_call x1, Pallas kernels, register(): pl.pallas_call(register_kernel, grid=(frames,), in_specs=[pl.BlockSpec(me...  9.29 us
    unnamed x32, local copies, waits for them, and re-layouts  7.47 us
  transfers between devices with their start and end apart: 11, of which 5 were waited for; matrix products, arithmetic and copies ran while one was open for 1% of the time, Pallas kernels for 3%

profile of v3, /device:TPU:1, one launch (start us, length us, event | category | flops | bytes accessed | tf_op | source)
XLA Modules:
  0.0 231.8 jit_solution(6517732995597543130)
XLA Ops:
  0.6 3.8 %pack_edges.1 = (bf16[512,128]{1,0:T(8,128)(2,1)}, bf16[512,128]{1,0:T(8,128)(2,1)}) custom-call(bf16[8,512,512]{2,1,0:T(8,128)(2,1)} %frame_ref.1, bf16[8,512,512]{2,1,0:T(8,128)(2,1)} %frame_ref.1), custom_call_target="tpu_custom_call" | custom-call | tf_op jit(solution)/shard_map/pack_edges/pallas_call | solution.py:56
  4.5 2.6 %collective-permute-start.1 = (bf16[512,128]{1,0:T(8,128)(2,1)}, bf16[512,128]{1,0:T(8,128)(2,1)S(1)}, u32[]{:S(2)}, u32[]{:S(2)}) collective-permute-start(bf16[512,128]{1,0:T(8,128)(2,1)} %get-tuple-element.19), channel_id=1, source_target_pairs={{0,1},{1,2},{2,3},{3,0},{4,5},{5,6},{6,7},{7,4},{8,9},{9,10},{10,1... | collective-permute-start | bytes 393224 | tf_op jit(solution)/shard_map/ppermute | solution.py:508
  7.2 3.6 %collective-permute-done.head_ref = bf16[512,128]{1,0:T(8,128)(2,1)S(1)} collective-permute-done((bf16[512,128]{1,0:T(8,128)(2,1)}, bf16[512,128]{1,0:T(8,128)(2,1)S(1)}, u32[]{:S(2)}, u32[]{:S(2)}) %collective-permute-start) | collective-permute-done | bytes 131104 | tf_op jit(solution)/shard_map/ppermute | solution.py:509
  10.7 9.3 %register.1 = (bf16[4,528,512]{2,1,0:T(8,128)(2,1)S(1)}, bf16[4,528,512]{2,1,0:T(8,128)(2,1)S(1)}) custom-call(s32[2,8]{1,0:T(2,128)S(1)} %constant_dynamic-slice_fusion.shifts_ref, bf16[8,512,512]{2,1,0:T(8,128)(2,1)} %frame_ref.1, bf16[512,128]{1,0:T(8,128)(2,1)S(1)} %collective-permute-done.head_ref, bf16[512,128]{1,0:T(8,128)(2,1)S(1)} %collective-permute-done.1.tail_ref), custom_call_target="tpu_custom_call" | custom-call | tf_op jit(solution)/shard_map/register/pallas_call | solution.py:126
  20.1 53.5 %all_to_all.10.recv_ref = bf16[4,528,512]{2,1,0:T(8,128)(2,1)} all-to-all(bf16[4,528,512]{2,1,0:T(8,128)(2,1)S(1)} %get-tuple-element.21), channel_id=1, replica_groups=mesh['parts'=2,'wide'=4,'narrow'=4] {'wide'}, dimensions={0} | all-to-all | bytes 4325376 | tf_op jit(solution)/shard_map/all_to_all | solution.py:513
  73.7 3.6 %all-to-all-start = ((bf16[4,528,512]{2,1,0:T(8,128)(2,1)}), bf16[4,528,512]{2,1,0:T(8,128)(2,1)S(1)}, u32[]{:S(2)}, u32[]{:S(2)}) async-start(bf16[4,528,512]{2,1,0:T(8,128)(2,1)} %copy-done.5), calls=%async_computation | async-start | bytes 4325376 | tf_op jit(solution)/shard_map/all_to_all | solution.py:513
  77.4 3.6 %collective-permute-start.3 = (f32[32,2]{1,0:T(8,128)S(1)}, f32[32,2]{1,0:T(8,128)S(1)}, u32[]{:S(2)}, u32[]{:S(2)}) collective-permute-start(f32[32,2]{1,0:T(8,128)S(1)} %convert_element_type.4), channel_id=1, source_target_pairs={{1,0},{2,1},{3,2},{5,4},{6,5},{7,6},{9,8},{10,9},{11,10},{13,12},{... | collective-permute-start | bytes 776 | tf_op jit(solution)/shard_map/ppermute | solution.py:494
  81.0 3.8 %collective-permute-start.2 = (f32[32,2]{1,0:T(8,128)S(1)}, f32[32,2]{1,0:T(8,128)S(1)}, u32[]{:S(2)}, u32[]{:S(2)}) collective-permute-start(f32[32,2]{1,0:T(8,128)S(1)} %convert_element_type.4), channel_id=1, source_target_pairs={{0,1},{1,2},{2,3},{4,5},{5,6},{6,7},{8,9},{9,10},{10,11},{12,13},{... | collective-permute-start | bytes 776 | tf_op jit(solution)/shard_map/ppermute | solution.py:493
  85.8 1.6 copy-done.4
  87.4 7.9 %observe.2 = (bf16[16,135168]{1,0:T(8,128)(2,1)}, f32[32,16]{1,0:T(8,128)}, f32[32,16]{1,0:T(8,128)S(1)}, f32[32,128]{1,0:T(8,128)S(1)}) custom-call(bf16[256,256]{1,0:T(8,128)(2,1)S(1)} %copy-done.6, bf16[4,528,512]{2,1,0:T(8,128)(2,1)S(1)} %copy-done.4, f32[8,4224]{1,0:T(8,128)S(1)} %stack.34.pattern_ref.refs_3_, ...), custom_call_target="tpu_custom_call" | custom-call | tf_op jit(solution)/shard_map/observe/pallas_call | solution.py:254
  95.3 31.1 %all-to-all-done.recv_ref = bf16[4,528,512]{2,1,0:T(8,128)(2,1)S(1)} async-done(((bf16[4,528,512]{2,1,0:T(8,128)(2,1)}), bf16[4,528,512]{2,1,0:T(8,128)(2,1)S(1)}, u32[]{:S(2)}, u32[]{:S(2)}) %all-to-all-start) | async-done | bytes 2162720 | tf_op jit(solution)/shard_map/all_to_all | solution.py:513
  126.4 7.9 %observe.3 = (bf16[16,135168]{1,0:T(8,128)(2,1)}, f32[32,16]{1,0:T(8,128)S(1)}, f32[32,16]{1,0:T(8,128)}, f32[32,128]{1,0:T(8,128)}) custom-call(bf16[256,256]{1,0:T(8,128)(2,1)S(1)} %copy-done.6, bf16[4,528,512]{2,1,0:T(8,128)(2,1)S(1)} %all-to-all-done.recv_ref, f32[8,4224]{1,0:T(8,128)S(1)} %stack.34.pattern_ref.refs_3_, ...), custom_call_target="tpu_custom_call", output_to_operand_aliasing={{0}: (6, {})} | custom-call | tf_op jit(solution)/shard_map/observe/pallas_call | solution.py:254
  134.2 3.4 %collective-permute-start.5 = (f32[32,16]{1,0:T(8,128)S(1)}, f32[32,16]{1,0:T(8,128)S(1)}, u32[]{:S(2)}, u32[]{:S(2)}) collective-permute-start(f32[32,16]{1,0:T(8,128)S(1)} %get-tuple-element.25.refs_0_), channel_id=1, source_target_pairs={{1,0},{2,1},{3,2},{5,4},{6,5},{7,6},{9,8},{10,9},{11,10},{13,12},{... | collective-permute-start | bytes 6152 | tf_op jit(solution)/shard_map/ppermute | solution.py:494
  137.6 4.0 %collective-permute-start.4 = (f32[32,16]{1,0:T(8,128)S(1)}, f32[32,16]{1,0:T(8,128)S(1)}, u32[]{:S(2)}, u32[]{:S(2)}) collective-permute-start(f32[32,16]{1,0:T(8,128)S(1)} %get-tuple-element.25.refs_0_), channel_id=1, source_target_pairs={{0,1},{1,2},{2,3},{4,5},{5,6},{6,7},{8,9},{9,10},{10,11},{12,13},{... | collective-permute-start | bytes 6152 | tf_op jit(solution)/shard_map/ppermute | solution.py:493
  141.6 0.8 collective-permute-done.4.refs_1_
  142.5 2.2 copy-done.2
  144.7 27.9 %sweep.3 = (f32[32,135168]{1,0:T(8,128)}, f32[32,36864]{1,0:T(8,128)}, f32[32,16]{1,0:T(8,128)S(1)}) custom-call(f32[32,16]{1,0:T(8,128)S(1)} %get-tuple-element.25.refs_0_, f32[32,16]{1,0:T(8,128)S(1)} %collective-permute-done.4.refs_1_, f32[32,16]{1,0:T(8,128)S(1)} %collective-permute-done.5.refs_2_, f32[8,4224]{1,0:T(8,128)S(1)} %stack.34.pattern_ref.refs_3_, ...), custom_call_target="tpu_custom_call" | custom-call | tf_op jit(solution)/shard_map/sweep/pallas_call | solution.py:479
  172.6 1.9 collective-permute-start.7
  174.5 4.4 %collective-permute-start.6 = (f32[32,16]{1,0:T(8,128)S(1)}, f32[32,16]{1,0:T(8,128)S(1)}, u32[]{:S(2)}, u32[]{:S(2)}) collective-permute-start(f32[32,16]{1,0:T(8,128)S(1)} %get-tuple-element.27.refs_0_), channel_id=1, source_target_pairs={{0,1},{1,2},{2,3},{4,5},{5,6},{6,7},{8,9},{9,10},{10,11},{12,13},{... | collective-permute-start | bytes 6152 | tf_op jit(solution)/shard_map/ppermute | solution.py:493
  179.5 27.0 %sweep.4 = (f32[32,135168]{1,0:T(8,128)}, f32[32,36864]{1,0:T(8,128)}, f32[32,16]{1,0:T(8,128)S(1)}) custom-call(f32[32,16]{1,0:T(8,128)S(1)} %get-tuple-element.27.refs_0_, f32[32,16]{1,0:T(8,128)S(1)} %collective-permute-done.6.refs_1_, f32[32,16]{1,0:T(8,128)S(1)} %collective-permute-done.7.refs_2_, f32[8,4224]{1,0:T(8,128)S(1)} %stack.34.pattern_ref.refs_3_, ...), custom_call_target="tpu_custom_call" | custom-call | tf_op jit(solution)/shard_map/sweep/pallas_call | solution.py:479
  206.5 1.9 collective-permute-start.9
  208.5 4.2 %collective-permute-start.8 = (f32[32,16]{1,0:T(8,128)S(1)}, f32[32,16]{1,0:T(8,128)S(1)}, u32[]{:S(2)}, u32[]{:S(2)}) collective-permute-start(f32[32,16]{1,0:T(8,128)S(1)} %get-tuple-element.30.refs_0_), channel_id=1, source_target_pairs={{0,1},{1,2},{2,3},{4,5},{5,6},{6,7},{8,9},{9,10},{10,11},{12,13},{... | collective-permute-start | bytes 6152 | tf_op jit(solution)/shard_map/ppermute | solution.py:493
  214.1 2.2 copy-done.3
  216.3 15.5 %sweep.5 = bf16[32,135168]{1,0:T(8,128)(2,1)} custom-call(f32[32,16]{1,0:T(8,128)S(1)} %get-tuple-element.30.refs_0_, f32[32,16]{1,0:T(8,128)S(1)} %collective-permute-done.8.refs_1_, f32[32,16]{1,0:T(8,128)S(1)} %collective-permute-done.9.refs_2_, f32[8,4224]{1,0:T(8,128)S(1)} %stack.34.pattern_ref.refs_3_, ...), custom_call_target="tpu_custom_call" | custom-call | tf_op jit(solution)/shard_map/sweep/pallas_call | solution.py:479
  (56 shorter events, 3.2 us)
Async XLA Ops:
  0.6 6.5 %copy-start = (s32[2,32]{1,0:T(2,128)S(1)}, s32[2,32]{1,0:T(2,128)}, u32[]{:S(2)}) copy-start(s32[2,32]{1,0:T(2,128)} %param.13) | copy-start | bytes 772
  4.4 6.3 %collective-permute-start = (bf16[512,128]{1,0:T(8,128)(2,1)}, bf16[512,128]{1,0:T(8,128)(2,1)S(1)}, u32[]{:S(2)}, u32[]{:S(2)}) collective-permute-start(bf16[512,128]{1,0:T(8,128)(2,1)} %get-tuple-element.18), channel_id=1, source_target_pairs={{1,0},{2,1},{3,2},{0,3},{5,4},{6,5},{7,6},{4,7},{9,8},{10,9},{11,1... | collective-permute-start | bytes 393224 | tf_op jit(solution)/shard_map/ppermute | solution.py:509
  4.5 6.2 %collective-permute-start.1 = (bf16[512,128]{1,0:T(8,128)(2,1)}, bf16[512,128]{1,0:T(8,128)(2,1)S(1)}, u32[]{:S(2)}, u32[]{:S(2)}) collective-permute-start(bf16[512,128]{1,0:T(8,128)(2,1)} %get-tuple-element.19), channel_id=1, source_target_pairs={{0,1},{1,2},{2,3},{3,0},{4,5},{5,6},{6,7},{7,4},{8,9},{9,10},{10,1... | collective-permute-start | bytes 393224 | tf_op jit(solution)/shard_map/ppermute | solution.py:508
  20.0 53.6 %copy-start.5 = (bf16[4,528,512]{2,1,0:T(8,128)(2,1)}, bf16[4,528,512]{2,1,0:T(8,128)(2,1)S(1)}, u32[]{:S(2)}) copy-start(bf16[4,528,512]{2,1,0:T(8,128)(2,1)S(1)} %get-tuple-element.20) | copy-start | bytes 6488068
  20.0 57.3 %copy-start.13 = (s32[1,1,32]{2,1,0:T(1,128)S(1)}, s32[1,1,32]{2,1,0:T(1,128)}, u32[]{:S(2)}) copy-start(s32[1,1,32]{2,1,0:T(1,128)} %param.15) | copy-start | bytes 388
  20.1 57.3 %copy-start.14 = (s32[1,1,32]{2,1,0:T(1,128)S(1)}, s32[1,1,32]{2,1,0:T(1,128)}, u32[]{:S(2)}) copy-start(s32[1,1,32]{2,1,0:T(1,128)} %param.14) | copy-start | bytes 388
  20.1 64.8 %copy-start.7 = (s32[4224]{0:T(1024)S(1)}, s32[4224]{0:T(1024)}, u32[]{:S(2)}) copy-start(s32[4224]{0:T(1024)} %constant.13.clone) | copy-start | bytes 50692
  20.1 64.8 %copy-start.8 = (f32[4224]{0:T(1024)S(1)}, f32[4224]{0:T(1024)}, u32[]{:S(2)}) copy-start(f32[4224]{0:T(1024)} %constant.41.clone) | copy-start | bytes 50692
  20.1 64.8 %copy-start.9 = (f32[4224]{0:T(1024)S(1)}, f32[4224]{0:T(1024)}, u32[]{:S(2)}) copy-start(f32[4224]{0:T(1024)} %constant.40.clone) | copy-start | bytes 50692
  20.1 65.0 %copy-start.10 = (f32[1,4224]{1,0:T(1,128)S(1)}, f32[1,4224]{1,0:T(1,128)}, u32[]{:S(2)}) copy-start(f32[1,4224]{1,0:T(1,128)} %constant.51) | copy-start | bytes 50692
  20.1 65.0 %copy-start.11 = (f32[1,4224]{1,0:T(1,128)S(1)}, f32[1,4224]{1,0:T(1,128)}, u32[]{:S(2)}) copy-start(f32[1,4224]{1,0:T(1,128)} %constant.50) | copy-start | bytes 50692
  20.1 65.6 %copy-start.6 = (bf16[256,256]{1,0:T(8,128)(2,1)S(1)}, bf16[256,256]{1,0:T(8,128)(2,1)}, u32[]{:S(2)}) copy-start(bf16[256,256]{1,0:T(8,128)(2,1)} %constant.44.clone.mix_ref) | copy-start | bytes 393220
  73.7 52.7 %all-to-all-start = ((bf16[4,528,512]{2,1,0:T(8,128)(2,1)}), bf16[4,528,512]{2,1,0:T(8,128)(2,1)S(1)}, u32[]{:S(2)}, u32[]{:S(2)}) async-start(bf16[4,528,512]{2,1,0:T(8,128)(2,1)} %copy-done.5), calls=%async_computation | async-start | bytes 4325376 | tf_op jit(solution)/shard_map/all_to_all | solution.py:513
  77.4 7.8 %collective-permute-start.3 = (f32[32,2]{1,0:T(8,128)S(1)}, f32[32,2]{1,0:T(8,128)S(1)}, u32[]{:S(2)}, u32[]{:S(2)}) collective-permute-start(f32[32,2]{1,0:T(8,128)S(1)} %convert_element_type.4), channel_id=1, source_target_pairs={{1,0},{2,1},{3,2},{5,4},{6,5},{7,6},{9,8},{10,9},{11,10},{13,12},{... | collective-permute-start | bytes 776 | tf_op jit(solution)/shard_map/ppermute | solution.py:494
  81.0 4.6 %collective-permute-start.2 = (f32[32,2]{1,0:T(8,128)S(1)}, f32[32,2]{1,0:T(8,128)S(1)}, u32[]{:S(2)}, u32[]{:S(2)}) collective-permute-start(f32[32,2]{1,0:T(8,128)S(1)} %convert_element_type.4), channel_id=1, source_target_pairs={{0,1},{1,2},{2,3},{4,5},{5,6},{6,7},{8,9},{9,10},{10,11},{12,13},{... | collective-permute-start | bytes 776 | tf_op jit(solution)/shard_map/ppermute | solution.py:493
  134.2 7.4 %collective-permute-start.5 = (f32[32,16]{1,0:T(8,128)S(1)}, f32[32,16]{1,0:T(8,128)S(1)}, u32[]{:S(2)}, u32[]{:S(2)}) collective-permute-start(f32[32,16]{1,0:T(8,128)S(1)} %get-tuple-element.25.refs_0_), channel_id=1, source_target_pairs={{1,0},{2,1},{3,2},{5,4},{6,5},{7,6},{9,8},{10,9},{11,10},{13,12},{... | collective-permute-start | bytes 6152 | tf_op jit(solution)/shard_map/ppermute | solution.py:494
  137.6 4.8 %collective-permute-start.4 = (f32[32,16]{1,0:T(8,128)S(1)}, f32[32,16]{1,0:T(8,128)S(1)}, u32[]{:S(2)}, u32[]{:S(2)}) collective-permute-start(f32[32,16]{1,0:T(8,128)S(1)} %get-tuple-element.25.refs_0_), channel_id=1, source_target_pairs={{0,1},{1,2},{2,3},{4,5},{5,6},{6,7},{8,9},{9,10},{10,11},{12,13},{... | collective-permute-start | bytes 6152 | tf_op jit(solution)/shard_map/ppermute | solution.py:493
  172.6 6.3 %collective-permute-start.7 = (f32[32,16]{1,0:T(8,128)S(1)}, f32[32,16]{1,0:T(8,128)S(1)}, u32[]{:S(2)}, u32[]{:S(2)}) collective-permute-start(f32[32,16]{1,0:T(8,128)S(1)} %get-tuple-element.27.refs_0_), channel_id=1, source_target_pairs={{1,0},{2,1},{3,2},{5,4},{6,5},{7,6},{9,8},{10,9},{11,10},{13,12},{... | collective-permute-start | bytes 6152 | tf_op jit(solution)/shard_map/ppermute | solution.py:494
  174.5 5.1 %collective-permute-start.6 = (f32[32,16]{1,0:T(8,128)S(1)}, f32[32,16]{1,0:T(8,128)S(1)}, u32[]{:S(2)}, u32[]{:S(2)}) collective-permute-start(f32[32,16]{1,0:T(8,128)S(1)} %get-tuple-element.27.refs_0_), channel_id=1, source_target_pairs={{0,1},{1,2},{2,3},{4,5},{5,6},{6,7},{8,9},{9,10},{10,11},{12,13},{... | collective-permute-start | bytes 6152 | tf_op jit(solution)/shard_map/ppermute | solution.py:493
  179.5 33.1 %copy-start.12 = (f32[1,1,32]{2,1,0:T(1,128)S(1)}, f32[1,1,32]{2,1,0:T(1,128)}, u32[]{:S(2)}) copy-start(f32[1,1,32]{2,1,0:T(1,128)} %param.16) | copy-start | bytes 388
  206.5 7.6 %collective-permute-start.9 = (f32[32,16]{1,0:T(8,128)S(1)}, f32[32,16]{1,0:T(8,128)S(1)}, u32[]{:S(2)}, u32[]{:S(2)}) collective-permute-start(f32[32,16]{1,0:T(8,128)S(1)} %get-tuple-element.30.refs_0_), channel_id=1, source_target_pairs={{1,0},{2,1},{3,2},{5,4},{6,5},{7,6},{9,8},{10,9},{11,10},{13,12},{... | collective-permute-start | bytes 6152 | tf_op jit(solution)/shard_map/ppermute | solution.py:494
  208.5 5.7 %collective-permute-start.8 = (f32[32,16]{1,0:T(8,128)S(1)}, f32[32,16]{1,0:T(8,128)S(1)}, u32[]{:S(2)}, u32[]{:S(2)}) collective-permute-start(f32[32,16]{1,0:T(8,128)S(1)} %get-tuple-element.30.refs_0_), channel_id=1, source_target_pairs={{0,1},{1,2},{2,3},{4,5},{5,6},{6,7},{8,9},{9,10},{10,11},{12,13},{... | collective-permute-start | bytes 6152 | tf_op jit(solution)/shard_map/ppermute | solution.py:493
  214.1 2.2 copy-start.3
  216.3 15.5 %copy-start.1 = (s32[2,32]{1,0:T(2,128)S(1)}, s32[2,32]{1,0:T(2,128)}, u32[]{:S(2)}) copy-start(s32[2,32]{1,0:T(2,128)} %param.13) | copy-start | bytes 772
  (2 other events, 3.8 us)

commit v4 on v3

--- a/solution.py
+++ b/solution.py
@@ -488,6 +488,52 @@
     )(*args)
 
 
+def exchange_kernel(count, traces_ref, left_ref, right_ref, landed, send_sem, recv_sem):
+    me = lax.axis_index("narrow")
+    right = lax.rem(me + 1, count)
+    left = lax.rem(me + count - 1, count)
+    barrier = pltpu.get_barrier_semaphore()
+    for other in (left, right):
+        pl.semaphore_signal(
+            barrier, inc=1, device_id={"narrow": other}, device_id_type=pl.DeviceIdType.MESH
+        )
+    pl.semaphore_wait(barrier, 2)
+    copies = []
+    for k, other in enumerate((right, left)):
+        copy = pltpu.make_async_remote_copy(
+            src_ref=traces_ref,
+            dst_ref=landed.at[k],
+            send_sem=send_sem.at[k],
+            recv_sem=recv_sem.at[k],
+            device_id={"narrow": other},
+            device_id_type=pl.DeviceIdType.MESH,
+        )
+        copy.start()
+        copies.append(copy)
+    for copy in copies:
+        copy.wait()
+    left_ref[...] = landed[0]
+    right_ref[...] = landed[1]
+
+
+def exchange(traces):
+    shape = jax.ShapeDtypeStruct(traces.shape, f32)
+    vmem = pl.BlockSpec(memory_space=pltpu.VMEM)
+    return pl.pallas_call(
+        functools.partial(exchange_kernel, lax.axis_size("narrow")),
+        in_specs=[vmem],
+        out_specs=[vmem, vmem],
+        out_shape=[shape, shape],
+        scratch_shapes=[
+            pltpu.VMEM((2,) + traces.shape, f32),
+            pltpu.SemaphoreType.DMA((2,)),
+            pltpu.SemaphoreType.DMA((2,)),
+        ],
+        compiler_params=pltpu.CompilerParams(collective_id=0, has_side_effects=True),
+        name="exchange",
+    )(traces)
+
+
 def from_neighbours(value, axis):
     count = lax.axis_size(axis)
     left = lax.ppermute(value, axis, [(i, i + 1) for i in range(count - 1)])
@@ -519,8 +565,10 @@
     col = place % ext_width - MARGIN
     global_col = lax.axis_index("narrow") * cols + jnp.asarray(col, jnp.int32)
     inside = ((global_col >= 0) & (global_col < cols * narrow)).astype(f32)
-    is_left = jnp.asarray(col < MARGIN, f32) * inside
-    is_right = jnp.asarray(col >= cols - MARGIN, f32) * inside
+    has_left = (lax.axis_index("narrow") > 0).astype(f32)
+    has_right = (lax.axis_index("narrow") < narrow - 1).astype(f32)
+    is_left = jnp.asarray(col < MARGIN, f32) * inside * has_left
+    is_right = jnp.asarray(col >= cols - MARGIN, f32) * inside * has_right
     zero = jnp.zeros_like(inside)
     pattern = jnp.stack(
         [jnp.asarray(row, f32), jnp.asarray(col, f32), inside, is_left, is_right, zero, zero, zero]
@@ -537,7 +585,7 @@
     observed, traces = earlier[:2]
     state = None
     for turn in range(ITERS):
-        left, right = from_neighbours(traces, "narrow")
+        left, right = exchange(traces)
         final = turn == ITERS - 1
         out = sweep(
             traces, left, right, pattern, centers, observed, state, rows_patch, cols, final

time: 233 us -> 240 us (1.030)
  starting transfers between devices: 33.4 us -> 13.6 us
  Pallas kernels: 99.2 us -> 115 us
  local copies, waits for them, and re-layouts: 7.96 us -> 19.2 us
    pallas_call x0 -> x3, Pallas kernels: none -> 15.5 us  [exchange(): pl.pallas_call(functools.partial(exchange_kernel, lax.axis_size('narrow')...]
    ppermute x4 -> x1, starting transfers between devices: 16.3 us -> 3.76 us  [from_neighbours(): left = lax.ppermute(value, axis, [(i, i + 1) for i in range(count - 1)])]
    unnamed x32 -> x58, local copies, waits for them, and re-layouts: 7.47 us -> 18.7 us
    ppermute x4 -> x1, starting transfers between devices: 10.8 us -> 3.61 us  [from_neighbours(): right = lax.ppermute(value, axis, [(i + 1, i) for i in range(count - 1)])]
  transfers between devices with their start and end apart: 11 -> 5, of which waited for: 5 -> 3; matrix products, arithmetic and copies ran while one was open for 1% -> 0% of each run, Pallas kernels for 3% -> 3%
where the time goes in v4:
time: 240 us; the launch traced here: 238 us
  Pallas kernels  115 us (48%)
  blocking collectives  53.5 us (22%)
  waiting for transfers between devices  35 us (15%)
  local copies, waits for them, and re-layouts  19.2 us (8%)
  starting transfers between devices  13.6 us (6%)
    pallas_call x3, Pallas kernels, sweep(): pl.pallas_call(functools.partial(sweep_kernel, rows_patch, cols, first, f...  70.4 us
    all_to_all x1, blocking collectives, shards(): lax.all_to_all(part, 'wide', split_axis=0, concat_axis=0, tiled=True)  53.5 us
    all_to_all x1, waiting for transfers between devices, shards(): lax.all_to_all(part, 'wide', split_axis=0, concat_axis=0, tiled=True)  31.1 us
    unnamed x58, local copies, waits for them, and re-layouts  18.7 us
    pallas_call x2, Pallas kernels, observe(): pl.pallas_call(functools.partial(observe_kernel, chunk, rows_chunk), grid...  15.8 us
    pallas_call x3, Pallas kernels, exchange(): pl.pallas_call(functools.partial(exchange_kernel, lax.axis_size('narrow')...  15.5 us
    pallas_call x1, Pallas kernels, register(): pl.pallas_call(register_kernel, grid=(frames,), in_specs=[pl.BlockSpec(me...  9.29 us
  transfers between devices with their start and end apart: 5, of which 3 were waited for; matrix products, arithmetic and copies ran while one was open for 0% of the time, Pallas kernels for 3%

profile of v4, /device:TPU:1, one launch (start us, length us, event | category | flops | bytes accessed | tf_op | source)
XLA Modules:
  0.0 238.0 jit_solution(8046589769874137517)
XLA Ops:
  0.6 3.8 %pack_edges.1 = (bf16[512,128]{1,0:T(8,128)(2,1)}, bf16[512,128]{1,0:T(8,128)(2,1)}) custom-call(bf16[8,512,512]{2,1,0:T(8,128)(2,1)} %frame_ref.1, bf16[8,512,512]{2,1,0:T(8,128)(2,1)} %frame_ref.1), custom_call_target="tpu_custom_call" | custom-call | tf_op jit(solution)/shard_map/pack_edges/pallas_call | solution.py:56
  4.5 2.6 %collective-permute-start.1 = (bf16[512,128]{1,0:T(8,128)(2,1)}, bf16[512,128]{1,0:T(8,128)(2,1)S(1)}, u32[]{:S(2)}, u32[]{:S(2)}) collective-permute-start(bf16[512,128]{1,0:T(8,128)(2,1)} %get-tuple-element.25), channel_id=1, source_target_pairs={{0,1},{1,2},{2,3},{3,0},{4,5},{5,6},{6,7},{7,4},{8,9},{9,10},{10,1... | collective-permute-start | bytes 393224 | tf_op jit(solution)/shard_map/ppermute | solution.py:554
  7.2 3.6 %collective-permute-done.head_ref = bf16[512,128]{1,0:T(8,128)(2,1)S(1)} collective-permute-done((bf16[512,128]{1,0:T(8,128)(2,1)}, bf16[512,128]{1,0:T(8,128)(2,1)S(1)}, u32[]{:S(2)}, u32[]{:S(2)}) %collective-permute-start) | collective-permute-done | bytes 131104 | tf_op jit(solution)/shard_map/ppermute | solution.py:555
  10.7 9.3 %register.1 = (bf16[4,528,512]{2,1,0:T(8,128)(2,1)S(1)}, bf16[4,528,512]{2,1,0:T(8,128)(2,1)S(1)}) custom-call(s32[2,8]{1,0:T(2,128)S(1)} %constant_dynamic-slice_fusion.shifts_ref, bf16[8,512,512]{2,1,0:T(8,128)(2,1)} %frame_ref.1, bf16[512,128]{1,0:T(8,128)(2,1)S(1)} %collective-permute-done.head_ref, bf16[512,128]{1,0:T(8,128)(2,1)S(1)} %collective-permute-done.1.tail_ref), custom_call_target="tpu_custom_call" | custom-call | tf_op jit(solution)/shard_map/register/pallas_call | solution.py:126
  20.1 53.5 %all_to_all.10.recv_ref = bf16[4,528,512]{2,1,0:T(8,128)(2,1)} all-to-all(bf16[4,528,512]{2,1,0:T(8,128)(2,1)S(1)} %get-tuple-element.27), channel_id=1, replica_groups=mesh['parts'=2,'wide'=4,'narrow'=4] {'wide'}, dimensions={0} | all-to-all | bytes 4325376 | tf_op jit(solution)/shard_map/all_to_all | solution.py:559
  73.7 3.6 %all-to-all-start = ((bf16[4,528,512]{2,1,0:T(8,128)(2,1)}), bf16[4,528,512]{2,1,0:T(8,128)(2,1)S(1)}, u32[]{:S(2)}, u32[]{:S(2)}) async-start(bf16[4,528,512]{2,1,0:T(8,128)(2,1)} %copy-done.6), calls=%async_computation | async-start | bytes 4325376 | tf_op jit(solution)/shard_map/all_to_all | solution.py:559
  77.4 3.6 %collective-permute-start.3 = (f32[32,2]{1,0:T(8,128)S(1)}, f32[32,2]{1,0:T(8,128)S(1)}, u32[]{:S(2)}, u32[]{:S(2)}) collective-permute-start(f32[32,2]{1,0:T(8,128)S(1)} %convert_element_type.12), channel_id=1, source_target_pairs={{1,0},{2,1},{3,2},{5,4},{6,5},{7,6},{9,8},{10,9},{11,10},{13,12},{... | collective-permute-start | bytes 776 | tf_op jit(solution)/shard_map/ppermute | solution.py:540
  81.0 3.8 %collective-permute-start.2 = (f32[32,2]{1,0:T(8,128)S(1)}, f32[32,2]{1,0:T(8,128)S(1)}, u32[]{:S(2)}, u32[]{:S(2)}) collective-permute-start(f32[32,2]{1,0:T(8,128)S(1)} %convert_element_type.12), channel_id=1, source_target_pairs={{0,1},{1,2},{2,3},{4,5},{5,6},{6,7},{8,9},{9,10},{10,11},{12,13},{... | collective-permute-start | bytes 776 | tf_op jit(solution)/shard_map/ppermute | solution.py:539
  85.8 1.6 copy-done.5
  87.4 7.9 %observe.2 = (bf16[16,135168]{1,0:T(8,128)(2,1)}, f32[32,16]{1,0:T(8,128)}, f32[32,16]{1,0:T(8,128)S(1)}, f32[32,128]{1,0:T(8,128)S(1)}) custom-call(bf16[256,256]{1,0:T(8,128)(2,1)S(1)} %copy-done.7, bf16[4,528,512]{2,1,0:T(8,128)(2,1)S(1)} %copy-done.5, f32[8,4224]{1,0:T(8,128)S(1)} %stack.34.pattern_ref.refs_3_, ...), custom_call_target="tpu_custom_call" | custom-call | tf_op jit(solution)/shard_map/observe/pallas_call | solution.py:254
  95.3 31.1 %all-to-all-done.recv_ref = bf16[4,528,512]{2,1,0:T(8,128)(2,1)S(1)} async-done(((bf16[4,528,512]{2,1,0:T(8,128)(2,1)}), bf16[4,528,512]{2,1,0:T(8,128)(2,1)S(1)}, u32[]{:S(2)}, u32[]{:S(2)}) %all-to-all-start) | async-done | bytes 2162720 | tf_op jit(solution)/shard_map/all_to_all | solution.py:559
  126.4 7.9 %observe.3 = (bf16[16,135168]{1,0:T(8,128)(2,1)}, f32[32,16]{1,0:T(8,128)S(1)}, f32[32,16]{1,0:T(8,128)}, f32[32,128]{1,0:T(8,128)}) custom-call(bf16[256,256]{1,0:T(8,128)(2,1)S(1)} %copy-done.7, bf16[4,528,512]{2,1,0:T(8,128)(2,1)S(1)} %all-to-all-done.recv_ref, f32[8,4224]{1,0:T(8,128)S(1)} %stack.34.pattern_ref.refs_3_, ...), custom_call_target="tpu_custom_call", output_to_operand_aliasing={{0}: (6, {})} | custom-call | tf_op jit(solution)/shard_map/observe/pallas_call | solution.py:254
  134.8 6.4 %exchange.3 = (f32[32,16]{1,0:T(8,128)}, f32[32,16]{1,0:T(8,128)}) custom-call(f32[32,16]{1,0:T(8,128)} %copy-done.10), custom_call_target="tpu_custom_call" | custom-call | tf_op jit(solution)/shard_map/exchange/pallas_call | solution.py:522
  141.3 2.2 copy-done.2
  143.5 0.7 copy-done.11
  145.7 27.9 %sweep.3 = (f32[32,135168]{1,0:T(8,128)}, f32[32,36864]{1,0:T(8,128)}, f32[32,16]{1,0:T(8,128)S(1)}) custom-call(f32[32,16]{1,0:T(8,128)S(1)} %copy-done.11, f32[32,16]{1,0:T(8,128)S(1)} %copy-done.16, f32[32,16]{1,0:T(8,128)S(1)} %copy-done.17, f32[8,4224]{1,0:T(8,128)S(1)} %stack.34.pattern_ref.refs_3_, ...), custom_call_target="tpu_custom_call" | custom-call | tf_op jit(solution)/shard_map/sweep/pallas_call | solution.py:479
  174.1 4.5 %exchange.4 = (f32[32,16]{1,0:T(8,128)}, f32[32,16]{1,0:T(8,128)}) custom-call(f32[32,16]{1,0:T(8,128)} %copy-done.12), custom_call_target="tpu_custom_call" | custom-call | tf_op jit(solution)/shard_map/exchange/pallas_call | solution.py:522
  178.7 2.2 copy-done.3
  183.0 27.1 %sweep.4 = (f32[32,135168]{1,0:T(8,128)}, f32[32,36864]{1,0:T(8,128)}, f32[32,16]{1,0:T(8,128)S(1)}) custom-call(f32[32,16]{1,0:T(8,128)S(1)} %copy-done.13, f32[32,16]{1,0:T(8,128)S(1)} %copy-done.18, f32[32,16]{1,0:T(8,128)S(1)} %copy-done.19, f32[8,4224]{1,0:T(8,128)S(1)} %stack.34.pattern_ref.refs_3_, ...), custom_call_target="tpu_custom_call" | custom-call | tf_op jit(solution)/shard_map/sweep/pallas_call | solution.py:479
  210.7 4.5 %exchange.5 = (f32[32,16]{1,0:T(8,128)}, f32[32,16]{1,0:T(8,128)}) custom-call(f32[32,16]{1,0:T(8,128)} %copy-done.8), custom_call_target="tpu_custom_call" | custom-call | tf_op jit(solution)/shard_map/exchange/pallas_call | solution.py:522
  215.2 1.4 copy.21
  216.6 0.9 maximum_bitcast_fusion
  218.2 2.2 copy-done.4
  222.5 15.5 %sweep.5 = bf16[32,135168]{1,0:T(8,128)(2,1)} custom-call(f32[32,16]{1,0:T(8,128)S(1)} %copy-done.9, f32[32,16]{1,0:T(8,128)S(1)} %copy-done.14, f32[32,16]{1,0:T(8,128)S(1)} %copy-done.15, f32[8,4224]{1,0:T(8,128)S(1)} %stack.34.pattern_ref.refs_3_, f32[32,128]{1,0:T(8,128)S(1)} %maximum_maximum_fusion.centers_ref.refs_4_, ...), custom_call_target="tpu_custom_call" | custom-call | tf_op jit(solution)/shard_map/sweep/pallas_call | solution.py:479
  (73 shorter events, 9.3 us)
Async XLA Ops:
  0.6 6.5 %copy-start = (s32[2,32]{1,0:T(2,128)S(1)}, s32[2,32]{1,0:T(2,128)}, u32[]{:S(2)}) copy-start(s32[2,32]{1,0:T(2,128)} %param.13) | copy-start | bytes 772
  4.4 6.3 %collective-permute-start = (bf16[512,128]{1,0:T(8,128)(2,1)}, bf16[512,128]{1,0:T(8,128)(2,1)S(1)}, u32[]{:S(2)}, u32[]{:S(2)}) collective-permute-start(bf16[512,128]{1,0:T(8,128)(2,1)} %get-tuple-element.24), channel_id=1, source_target_pairs={{1,0},{2,1},{3,2},{0,3},{5,4},{6,5},{7,6},{4,7},{9,8},{10,9},{11,1... | collective-permute-start | bytes 393224 | tf_op jit(solution)/shard_map/ppermute | solution.py:555
  4.5 6.2 %collective-permute-start.1 = (bf16[512,128]{1,0:T(8,128)(2,1)}, bf16[512,128]{1,0:T(8,128)(2,1)S(1)}, u32[]{:S(2)}, u32[]{:S(2)}) collective-permute-start(bf16[512,128]{1,0:T(8,128)(2,1)} %get-tuple-element.25), channel_id=1, source_target_pairs={{0,1},{1,2},{2,3},{3,0},{4,5},{5,6},{6,7},{7,4},{8,9},{9,10},{10,1... | collective-permute-start | bytes 393224 | tf_op jit(solution)/shard_map/ppermute | solution.py:554
  20.0 53.6 %copy-start.6 = (bf16[4,528,512]{2,1,0:T(8,128)(2,1)}, bf16[4,528,512]{2,1,0:T(8,128)(2,1)S(1)}, u32[]{:S(2)}) copy-start(bf16[4,528,512]{2,1,0:T(8,128)(2,1)S(1)} %get-tuple-element.26) | copy-start | bytes 6488068
  20.0 57.3 %copy-start.26 = (s32[1,1,32]{2,1,0:T(1,128)S(1)}, s32[1,1,32]{2,1,0:T(1,128)}, u32[]{:S(2)}) copy-start(s32[1,1,32]{2,1,0:T(1,128)} %param.15) | copy-start | bytes 388
  20.1 57.3 %copy-start.27 = (s32[1,1,32]{2,1,0:T(1,128)S(1)}, s32[1,1,32]{2,1,0:T(1,128)}, u32[]{:S(2)}) copy-start(s32[1,1,32]{2,1,0:T(1,128)} %param.14) | copy-start | bytes 388
  20.1 64.8 %copy-start.20 = (s32[4224]{0:T(1024)S(1)}, s32[4224]{0:T(1024)}, u32[]{:S(2)}) copy-start(s32[4224]{0:T(1024)} %constant.14.clone) | copy-start | bytes 50692
  20.1 64.8 %copy-start.21 = (f32[4224]{0:T(1024)S(1)}, f32[4224]{0:T(1024)}, u32[]{:S(2)}) copy-start(f32[4224]{0:T(1024)} %constant.43.clone) | copy-start | bytes 50692
  20.1 64.8 %copy-start.22 = (f32[4224]{0:T(1024)S(1)}, f32[4224]{0:T(1024)}, u32[]{:S(2)}) copy-start(f32[4224]{0:T(1024)} %constant.42.clone) | copy-start | bytes 50692
  20.1 65.0 %copy-start.23 = (f32[1,4224]{1,0:T(1,128)S(1)}, f32[1,4224]{1,0:T(1,128)}, u32[]{:S(2)}) copy-start(f32[1,4224]{1,0:T(1,128)} %constant.53) | copy-start | bytes 50692
  20.1 65.0 %copy-start.24 = (f32[1,4224]{1,0:T(1,128)S(1)}, f32[1,4224]{1,0:T(1,128)}, u32[]{:S(2)}) copy-start(f32[1,4224]{1,0:T(1,128)} %constant.52) | copy-start | bytes 50692
  20.1 65.6 %copy-start.7 = (bf16[256,256]{1,0:T(8,128)(2,1)S(1)}, bf16[256,256]{1,0:T(8,128)(2,1)}, u32[]{:S(2)}) copy-start(bf16[256,256]{1,0:T(8,128)(2,1)} %constant.46.clone.mix_ref) | copy-start | bytes 393220
  73.7 52.7 %all-to-all-start = ((bf16[4,528,512]{2,1,0:T(8,128)(2,1)}), bf16[4,528,512]{2,1,0:T(8,128)(2,1)S(1)}, u32[]{:S(2)}, u32[]{:S(2)}) async-start(bf16[4,528,512]{2,1,0:T(8,128)(2,1)} %copy-done.6), calls=%async_computation | async-start | bytes 4325376 | tf_op jit(solution)/shard_map/all_to_all | solution.py:559
  77.4 7.9 %collective-permute-start.3 = (f32[32,2]{1,0:T(8,128)S(1)}, f32[32,2]{1,0:T(8,128)S(1)}, u32[]{:S(2)}, u32[]{:S(2)}) collective-permute-start(f32[32,2]{1,0:T(8,128)S(1)} %convert_element_type.12), channel_id=1, source_target_pairs={{1,0},{2,1},{3,2},{5,4},{6,5},{7,6},{9,8},{10,9},{11,10},{13,12},{... | collective-permute-start | bytes 776 | tf_op jit(solution)/shard_map/ppermute | solution.py:540
  81.0 4.6 %collective-permute-start.2 = (f32[32,2]{1,0:T(8,128)S(1)}, f32[32,2]{1,0:T(8,128)S(1)}, u32[]{:S(2)}, u32[]{:S(2)}) collective-permute-start(f32[32,2]{1,0:T(8,128)S(1)} %convert_element_type.12), channel_id=1, source_target_pairs={{0,1},{1,2},{2,3},{4,5},{5,6},{6,7},{8,9},{9,10},{10,11},{12,13},{... | collective-permute-start | bytes 776 | tf_op jit(solution)/shard_map/ppermute | solution.py:539
  85.8 1.6 copy-start.5
  141.3 2.2 copy-start.2
  144.2 0.7 copy-start.16
  178.7 2.2 copy-start.3
  182.3 0.7 copy-start.19
  183.0 33.6 %copy-start.25 = (f32[1,1,32]{2,1,0:T(1,128)S(1)}, f32[1,1,32]{2,1,0:T(1,128)}, u32[]{:S(2)}) copy-start(f32[1,1,32]{2,1,0:T(1,128)} %param.16) | copy-start | bytes 388
  218.2 2.2 copy-start.4
  221.1 0.7 copy-start.14
  222.5 15.5 %copy-start.1 = (s32[2,32]{1,0:T(2,128)S(1)}, s32[2,32]{1,0:T(2,128)}, u32[]{:S(2)}) copy-start(s32[2,32]{1,0:T(2,128)} %param.13) | copy-start | bytes 772
  (9 other events, 6.1 us)
